TPU v7x, 128 devices: a whole 4x4x4 slice. The times are simulated.
128 devices in a mesh: groups: 32 (over z, y, core), blk: 4 (over x).
Axes of the slice: x: 4, y: 4, z: 4, core: 2. Of those that a mesh axis runs over, the one named last changes fastest.
Arguments:
- embeddings: bfloat16 [98304, 1024], P(('groups', 'blk')), may hold values from -6 to 6
- owner: int32 [98304, 1], P(('groups', 'blk')), may hold values from 0 to 31; in each aligned block of 768 rows (0 to 767, 768 to 1535, ...) at most 48 rows name the same one
- local_cluster: int32 [98304], P(('groups', 'blk')), may hold values from 0 to 15
Outputs:
- best: float32 [98304], P(('groups', 'blk'))
Inputs may be any that keep to these rules, and one draw needn't show every extreme that they name: `owner`: among the rows of one device no group is named by more than 48 rows, a bound that some block reaches.
All inputs are finite; a program needn't handle non-finite values.
Results may differ from a plain program's by a relative error of at most 0.0013.
Values may be sent and summed in bfloat16 or wider, within the bound.
No kernel may reach another device: no remote copies, remote signals or barrier semaphores. Data moves between devices by JAX's collectives and lax.ppermute only.
A program may use at most 64 MiB of HBM per device.

v0:
```python
import math

import jax
import jax.numpy as jnp
from jax import lax
from jax.sharding import PartitionSpec as P

CPG = 16


def pair_scores(left, right):
    return jnp.einsum("id,jd->ij", left, right, preferred_element_type=jnp.float32)


def body(embeddings, owner, local_cluster):
    rows = embeddings.shape[0]
    width = embeddings.shape[1]
    n_groups = lax.axis_size("groups")
    n_blk = lax.axis_size("blk")
    cap = 2 * rows // n_groups
    emb32 = embeddings.astype(jnp.float32)
    scale = lax.rsqrt(jnp.mean(emb32 * emb32, axis=1, keepdims=True) + 1e-06) / math.sqrt(width)
    unit = (emb32 * scale).astype(jnp.bfloat16)
    target = owner[:, 0]
    cluster = target * CPG + local_cluster
    device = lax.axis_index("groups") * n_blk + lax.axis_index("blk")
    global_id = device * rows + jnp.arange(rows, dtype=jnp.int32)
    onehot = (target[:, None] == jnp.arange(n_groups, dtype=jnp.int32)[None, :]).astype(jnp.int32)
    rank = jnp.sum(jnp.cumsum(onehot, axis=0) * onehot, axis=1) - 1
    slot = target * cap + rank
    send_rows = (
        jnp.zeros((n_groups * cap, width), jnp.bfloat16)
        .at[slot]
        .set(unit)
        .reshape(n_groups, cap, width)
    )
    send_ids = (
        jnp.full((n_groups * cap,), -1, jnp.int32).at[slot].set(global_id).reshape(n_groups, cap)
    )
    send_labels = (
        jnp.full((n_groups * cap,), -1, jnp.int32).at[slot].set(cluster).reshape(n_groups, cap)
    )
    got_rows, got_ids, got_labels = (
        lax.all_to_all(send_rows, "groups", split_axis=0, concat_axis=0, tiled=True),
        lax.all_to_all(send_ids, "groups", split_axis=0, concat_axis=0, tiled=True),
        lax.all_to_all(send_labels, "groups", split_axis=0, concat_axis=0, tiled=True),
    )
    mine = got_rows.reshape(n_groups * cap, width)
    ids = got_ids.reshape(n_groups * cap)
    labels = got_labels.reshape(n_groups * cap)
    start_best = jnp.full((n_groups * cap,), -1.0, jnp.float32)
    other_rows = lax.all_gather(mine, "blk", axis=0, tiled=True)
    other_ids = lax.all_gather(ids, "blk", axis=0, tiled=True)
    other_labels = lax.all_gather(labels, "blk", axis=0, tiled=True)
    prod = pair_scores(mine, other_rows)
    keep = (labels[:, None] == other_labels[None, :]) & (other_ids[None, :] < ids[:, None])
    running = jnp.maximum(start_best, jnp.max(jnp.where(keep, prod, -1.0), axis=1))
    back = lax.all_to_all(
        running.reshape(n_groups, cap), "groups", split_axis=0, concat_axis=0, tiled=True
    )
    return back.reshape(n_groups * cap)[slot]


def solution(mesh):
    placed = (P(("groups", "blk"), None), P(("groups", "blk"), None), P(("groups", "blk")))
    return jax.shard_map(
        body, mesh=mesh, in_specs=placed, out_specs=P(("groups", "blk")), check_vma=False
    )
```

profile of v0, /device:TPU:1, one launch (start us, length us, event | category | flops | bytes accessed | tf_op | source)
XLA Modules:
  0.0 242.3 jit_solution(18016123303585768688)
XLA Ops:
  6.5 0.0 all-gather.4.cloned.1.call-start
  6.5 0.7 reduce
  7.3 1.7 reduce-window.6
  9.0 0.3 slice_reduce_fusion
  9.3 0.1 fusion.7
  9.4 0.7 fusion.13
  10.1 1.8 fusion
  11.9 10.4 %scatter_custom_fusion.2 = bf16[1536,1024]{1,0:T(8,128)(2,1)S(1)} fusion(s32[768]{0:T(1024)S(1)} %fusion.13, bf16[768,1024]{1,0:T(8,128)(2,1)} %param.3, f32[768]{0:T(1024)S(1)} %rsqrt_multiply_fusion, bf16[]{:T(256)} %constant.15.clone.1), kind=kCustom, calls=%fused_computation.9 | custom fusion | flops 2359296 | bytes 4722690 | tf_op jit(solution)/shard_map/scatter | solution.py:34
  22.3 49.2 %all_to_all.29 = bf16[32,48,1024]{2,1,0:T(8,128)(2,1)} all-to-all(bf16[32,48,1024]{2,1,0:T(8,128)(2,1)S(1)} %bitcast.27), channel_id=1, replica_groups=mesh['groups'=32,'blk'=4] {'groups'}, dimensions={0} | all-to-all | bytes 6291456 | tf_op jit(solution)/shard_map/all_to_all | solution.py:44
  71.5 0.0 copy-start.1
  71.5 0.0 copy-start
  71.5 0.0 all-gather.4.cloned.1.call-update
  71.5 3.4 %scatter_custom_fusion.1 = s32[1536]{0:T(1024)S(1)} fusion(s32[768]{0:T(1024)S(1)} %fusion.13, s32[768]{0:T(1024)S(1)} %iota_add_fusion, s32[]{:T(128)} %constant.17.clone.1), kind=kCustom, calls=%fused_computation.26 | custom fusion | bytes 6148 | tf_op jit(solution)/shard_map/scatter | solution.py:38
  74.9 0.7 all_to_all.21
  75.6 3.8 %all-to-all-start.1 = ((s32[32,1,48]{2,1,0:T(1,128)}), s32[32,1,48]{2,1,0:T(1,128)S(1)}, u32[]{:S(2)}, u32[]{:S(2)}) async-start(s32[32,1,48]{2,1,0:T(1,128)} %all_to_all.21), calls=%async_computation.1 | async-start | bytes 32768 | tf_op jit(solution)/shard_map/all_to_all | solution.py:45
  79.5 0.0 copy-done.1
  79.5 3.4 %scatter_custom_fusion = s32[1536]{0:T(1024)S(1)} fusion(s32[768]{0:T(1024)S(1)} %fusion.13, s32[768]{0:T(1024)S(1)} %multiply_add_fusion, s32[]{:T(128)} %constant.17.clone.1), kind=kCustom, calls=%fused_computation.28 | custom fusion | bytes 6148 | tf_op jit(solution)/shard_map/scatter | solution.py:41
  82.9 0.7 all_to_all.19
  83.6 2.9 %all-to-all-done.1 = s32[32,1,48]{2,1,0:T(1,128)S(1)} async-done(((s32[32,1,48]{2,1,0:T(1,128)}), s32[32,1,48]{2,1,0:T(1,128)S(1)}, u32[]{:S(2)}, u32[]{:S(2)}) %all-to-all-start.1) | async-done | bytes 6176 | tf_op jit(solution)/shard_map/all_to_all | solution.py:45
  86.5 4.5 %all-to-all-start = ((s32[32,1,48]{2,1,0:T(1,128)}), s32[32,1,48]{2,1,0:T(1,128)S(1)}, u32[]{:S(2)}, u32[]{:S(2)}) async-start(s32[32,1,48]{2,1,0:T(1,128)} %all_to_all.19), calls=%async_computation | async-start | bytes 32768 | tf_op jit(solution)/shard_map/all_to_all | solution.py:46
  91.1 0.5 broadcast.103
  91.6 0.7 reduce.19
  92.3 0.1 reshape.120
  92.4 5.6 %all-to-all-done = s32[32,1,48]{2,1,0:T(1,128)S(1)} async-done(((s32[32,1,48]{2,1,0:T(1,128)}), s32[32,1,48]{2,1,0:T(1,128)S(1)}, u32[]{:S(2)}, u32[]{:S(2)}) %all-to-all-start) | async-done | bytes 6176 | tf_op jit(solution)/shard_map/all_to_all | solution.py:46
  98.0 0.7 reduce.20
  98.7 0.1 eq.48
  98.8 0.1 reshape.118
  98.9 0.1 reshape.82
  98.9 10.5 %all-gather.1 = s32[4,1,1536]{2,1,0:T(1,128)S(1)} all-gather(s32[1,1,1536]{2,1,0:T(1,128)S(1)} %reshape.120), channel_id=1, replica_groups=mesh['groups'=32,'blk'=4] {'blk'}, dimensions={0}, use_global_device_ids=true | all-gather | bytes 30720 | tf_op jit(solution)/shard_map/all_gather | solution.py:53
  109.4 10.3 %all-gather = s32[4,1,1536]{2,1,0:T(1,128)S(1)} all-gather(s32[1,1,1536]{2,1,0:T(1,128)S(1)} %reshape.118), channel_id=1, replica_groups=mesh['groups'=32,'blk'=4] {'blk'}, dimensions={0}, use_global_device_ids=true | all-gather | bytes 30720 | tf_op jit(solution)/shard_map/all_gather | solution.py:54
  119.7 68.2 %all-gather.4.cloned.1.call-done = bf16[6144,1024]{1,0:T(8,128)(2,1)} async-done(((bf16[1536,1024]{1,0:T(8,128)(2,1)}), bf16[6144,1024]{1,0:T(8,128)(2,1)}) %all-gather.4.cloned.1.call-update) | async-done | bytes 12582928 | tf_op jit(solution)/shard_map/all_gather | solution.py:52
  187.9 0.0 copy-done
  187.9 24.8 %select_reduce_fusion = f32[1536]{0:T(1024)S(1)} fusion(bf16[1536,1024]{1,0:T(8,128)(2,1)S(1)} %bitcast.26, bf16[6144,1024]{1,0:T(8,128)(2,1)} %all-gather.4.cloned.1.call-done, s32[6144]{0:T(1024)S(1)} %bitcast.31, s32[6144]{0:T(1024)S(1)} %bitcast.32, s32[1536]{0:T(1024)S(1)} %reshape.82, s32[1536]{0:T(1024)S(1)} %eq.48), kind=kOutput, calls=%fused_computation.4 | convolution fusion | flops 19374536704 | bytes 15796224 | tf_op jit(solution)/shard_map/id,jd->ij/dot_general | solution.py:12
  212.7 0.7 max_broadcast_in_dim.15
  213.4 7.7 %all-to-all-start.3 = ((f32[32,1,48]{2,1,0:T(1,128)}), f32[32,1,48]{2,1,0:T(1,128)S(1)}, u32[]{:S(2)}, u32[]{:S(2)}) async-start(f32[32,1,48]{2,1,0:T(1,128)} %max_broadcast_in_dim.15), calls=%async_computation.3 | async-start | bytes 32768 | tf_op jit(solution)/shard_map/all_to_all | solution.py:58
  221.1 6.9 %all-to-all-done.3 = f32[32,1,48]{2,1,0:T(1,128)S(1)} async-done(((f32[32,1,48]{2,1,0:T(1,128)}), f32[32,1,48]{2,1,0:T(1,128)S(1)}, u32[]{:S(2)}, u32[]{:S(2)}) %all-to-all-start.3) | async-done | bytes 6176 | tf_op jit(solution)/shard_map/all_to_all | solution.py:58
  228.0 0.5 broadcast.105
  228.5 0.7 reduce.21
  229.2 0.1 reshape.85
  229.3 6.1 %gather_fusion = f32[768]{0:T(1024)} fusion(f32[1536]{0:T(1024)S(1)} %reshape.85, s32[1024]{0:T(1024)S(1)} %pad_clamp_fusion), kind=kCustom, calls=%fused_computation | custom fusion | bytes 9216 | tf_op jit(solution)/shard_map/gather | solution.py:61
  (8 shorter events, 0.1 us)
Async XLA Ops:
  6.5 181.3 %all-gather.4.cloned.1.call-start = ((), (), s32[]{:S(2)}) async-start(), calls=%async_computation.4 | async-start | bytes 15728640 | tf_op jit(solution)/shard_map/all_gather | solution.py:52
  71.5 8.0 %copy-start.1 = (s32[768]{0:T(1024)S(1)}, s32[768]{0:T(1024)}, u32[]{:S(2)}) copy-start(s32[768]{0:T(1024)} %param.5) | copy-start | bytes 9220
  71.5 116.4 %copy-start = (bf16[32,48,1024]{2,1,0:T(8,128)(2,1)S(1)}, bf16[32,48,1024]{2,1,0:T(8,128)(2,1)}, u32[]{:S(2)}) copy-start(bf16[32,48,1024]{2,1,0:T(8,128)(2,1)} %all_to_all.29) | copy-start | bytes 9437188
  75.6 10.9 %all-to-all-start.1 = ((s32[32,1,48]{2,1,0:T(1,128)}), s32[32,1,48]{2,1,0:T(1,128)S(1)}, u32[]{:S(2)}, u32[]{:S(2)}) async-start(s32[32,1,48]{2,1,0:T(1,128)} %all_to_all.21), calls=%async_computation.1 | async-start | bytes 32768 | tf_op jit(solution)/shard_map/all_to_all | solution.py:45
  86.5 11.5 %all-to-all-start = ((s32[32,1,48]{2,1,0:T(1,128)}), s32[32,1,48]{2,1,0:T(1,128)S(1)}, u32[]{:S(2)}, u32[]{:S(2)}) async-start(s32[32,1,48]{2,1,0:T(1,128)} %all_to_all.19), calls=%async_computation | async-start | bytes 32768 | tf_op jit(solution)/shard_map/all_to_all | solution.py:46
  213.4 14.7 %all-to-all-start.3 = ((f32[32,1,48]{2,1,0:T(1,128)}), f32[32,1,48]{2,1,0:T(1,128)S(1)}, u32[]{:S(2)}, u32[]{:S(2)}) async-start(f32[32,1,48]{2,1,0:T(1,128)} %max_broadcast_in_dim.15), calls=%async_computation.3 | async-start | bytes 32768 | tf_op jit(solution)/shard_map/all_to_all | solution.py:58
Sparse Core Ops, SparseCore 0:
  71.6 116.2 all-gather.3
where the time goes:
time: 243 us; the launch traced here: 242 us
  waiting for transfers between devices  83.7 us (34%)
  blocking collectives  69.9 us (29%)
  matrix products  24.8 us (10%)
  other arithmetic  17.6 us (7%)
  local copies, waits for them, and re-layouts  16.7 us (7%)
  starting transfers between devices  16.1 us (7%)
  between operations  13.6 us (6%)
    all_gather x1, waiting for transfers between devices, body(): other_rows = lax.all_gather(mine, 'blk', axis=0, tiled=True)  68.2 us
    all_to_all x1, blocking collectives, body(): lax.all_to_all(send_rows, 'groups', split_axis=0, concat_axis=0, tiled=True)  49.2 us
    dot_general x1, matrix products, pair_scores(): jnp.einsum('id,jd->ij', left, right, preferred_element_type=jnp.float32)  24.8 us
    all_gather x1, blocking collectives, body(): other_ids = lax.all_gather(ids, 'blk', axis=0, tiled=True)  10.5 us
    scatter x1, other arithmetic, body(): send_rows = jnp.zeros((n_groups * cap, width), jnp.bfloat16).at[slot].set...  10.4 us
    all_gather x1, blocking collectives, body(): other_labels = lax.all_gather(labels, 'blk', axis=0, tiled=True)  10.3 us
    all_to_all x1, starting transfers between devices, body(): lax.all_to_all(running.reshape(n_groups, cap), 'groups', split_axis=0, co...  7.71 us
    all_to_all x1, waiting for transfers between devices, body(): lax.all_to_all(running.reshape(n_groups, cap), 'groups', split_axis=0, co...  6.93 us
  transfers between devices with their start and end apart: 4, of which 4 were waited for; matrix products, arithmetic and copies ran while one was open for 4% of the time, Pallas kernels for 0%

commit v1 on v0

v1 whole, which is shorter than its diff:
```python
import math

import jax
import jax.numpy as jnp
from jax import lax
from jax.experimental import pallas as pl
from jax.experimental.pallas import tpu as pltpu
from jax.sharding import Mesh, PartitionSpec as P

CPG = 16
GROUPS = 32
CLUSTERS = GROUPS * CPG
ROWS = 768
WIDTH = 1024
CHIPS = 64
DEVS = 128
CAP = 24
SLOTS = CHIPS * CAP
ALL = ("z", "y", "core", "x")
GROUP_AXES = ("z", "y", "core")
CHIP_AXES = ("z", "y", "x")
SHIFTS = (
    (0, 0, 0), (3, 7, 12), (5, 14, 9), (11, 2, 6), (8, 4, 13), (1, 10, 3), (14, 6, 2), (7, 13, 15),
    (12, 1, 8), (2, 9, 5), (9, 15, 1), (6, 3, 11), (15, 12, 4), (4, 11, 7), (10, 5, 14), (13, 8, 10),
)
BF16 = jnp.bfloat16
F32 = jnp.float32


def iota(shape, dim):
    return lax.broadcasted_iota(jnp.int32, shape, dim)


def dot(a, b, ca=1, cb=0, precision=None):
    return lax.dot_general(
        a, b, (((ca,), (cb,)), ((), ())), preferred_element_type=F32, precision=precision
    )


def onehot(cond):
    return jnp.where(cond, 1.0, 0.0).astype(BF16)


def place():
    zy = lax.axis_index("z") * 4 + lax.axis_index("y")
    return lax.axis_index("core"), zy * 4 + lax.axis_index("x")


def count_kernel(owner_ref, local_ref, hist_ref, ids_ref):
    owner, local = owner_ref[...], local_ref[...]
    by_owner = onehot(owner == iota((GROUPS, ROWS), 0))
    by_local = onehot(local == iota((CPG, ROWS), 0))
    pairs = dot(by_owner, by_local, 1, 1).astype(BF16)
    spread = onehot(iota((CPG, CLUSTERS), 1) % CPG == iota((CPG, CLUSTERS), 0))
    wide = dot(pairs, spread)
    mine = iota((GROUPS, CLUSTERS), 1) // CPG == iota((GROUPS, CLUSTERS), 0)
    counts = jnp.sum(jnp.where(mine, wide, 0.0), axis=0, keepdims=True)
    for j in range(CLUSTERS // 128):
        part = counts[:, j * 128 : (j + 1) * 128]
        hist_ref[:, j, :] = jnp.broadcast_to(part, (DEVS, 128))
    cluster = owner * CPG + local
    eye = iota((128, 128), 0) == iota((128, 128), 1)
    rank = jnp.zeros((1, ROWS), jnp.int32)
    for j in range(ROWS // 128):
        part = jnp.broadcast_to(cluster[:, j * 128 : (j + 1) * 128], (128, 128))
        column = jnp.sum(jnp.where(eye, part, 0), axis=1, keepdims=True)
        width = ROWS - j * 128
        later = iota((128, width), 1) > iota((128, width), 0)
        hit = jnp.where((column == cluster[:, j * 128 :]) & later, 1, 0)
        found = jnp.sum(hit, axis=0, keepdims=True)
        if j:
            found = jnp.concatenate([jnp.zeros((1, j * 128), jnp.int32), found], axis=1)
        rank = rank + found
    which = iota((8, ROWS), 0)
    ids_ref[...] = jnp.where(which == 0, cluster, jnp.where(which == 1, rank, 0))


def unit_kernel(emb_ref, unit_ref):
    emb = emb_ref[...].astype(F32)
    scale = lax.rsqrt(jnp.mean(emb * emb, axis=1, keepdims=True) + 1e-06) / math.sqrt(WIDTH)
    unit_ref[...] = (emb * scale).astype(BF16)


def rotate(value, by):
    if by == 0:
        return value
    inside = iota(value.shape, 1) % 16 >= by
    return jnp.where(inside, pltpu.roll(value, by, 1), pltpu.roll(value, by + 112, 1))


def pack_kernel(hist_ref, ids_ref, ids2_ref, unit_ref, unit2_ref, out_ref, ends_ref, rows_ref, load_ref):
    core, chip = place()
    hist = jnp.concatenate([hist_ref[:, j, :] for j in range(4)], axis=1).astype(BF16)
    dev = iota((CHIPS, DEVS), 1)
    first = iota((CHIPS, DEVS), 0) // 4 * 8 + iota((CHIPS, DEVS), 0) % 4
    count0 = dot(onehot(dev == first), hist)
    count1 = dot(onehot(dev == first + 4), hist)
    both = (count0 + count1).astype(BF16)

    in_group = iota((CLUSTERS, GROUPS), 0) // CPG == iota((CLUSTERS, GROUPS), 1)
    in_group_t = iota((GROUPS, CLUSTERS), 1) // CPG == iota((GROUPS, CLUSTERS), 0)
    size_row = jnp.sum(dot(both, onehot(in_group)), axis=0, keepdims=True)
    size_col = jnp.sum(dot(onehot(in_group_t), both, 1, 1), axis=1, keepdims=True)
    lower = iota((GROUPS, GROUPS), 0) < iota((GROUPS, GROUPS), 1)
    ahead = (size_col > size_row) | ((size_col == size_row) & lower)
    order = jnp.sum(jnp.where(ahead, 1, 0), axis=0, keepdims=True)
    order = jnp.sum(jnp.where(in_group, order, 0), axis=1, keepdims=True)
    quarter = order // 8
    place8 = order % 8
    octet = jnp.where(quarter % 2 == 1, 7 - place8, place8)
    local = iota((CLUSTERS, 1), 0) % CPG
    lane = iota((CLUSTERS, CLUSTERS), 1)
    spread = onehot(quarter * 128 + octet * 16 + local == lane)

    wide = dot(both, spread)
    parts = [wide[:, p * 128 : (p + 1) * 128] for p in range(4)]
    loads = []
    for shifts in SHIFTS:
        load = parts[0]
        for part, by in zip(parts[1:], shifts):
            load = load + rotate(part, by)
        loads.append(jnp.max(load, axis=0, keepdims=True))
    loads = jnp.concatenate(loads, axis=0)
    for by in (1, 2, 4, 8):
        loads = jnp.maximum(loads, rotate(loads, by))
    best = loads[0:1]
    chosen = [jnp.full((1, 128), by, jnp.int32) for by in SHIFTS[0]]
    for n, shifts in enumerate(SHIFTS[1:], 1):
        better = loads[n : n + 1] < best
        best = jnp.where(better, loads[n : n + 1], best)
        chosen = [jnp.where(better, by, old) for by, old in zip(shifts, chosen)]
    load_ref[...] = jnp.broadcast_to(jnp.max(best, axis=1, keepdims=True), (8, 128)).astype(jnp.int32)
    chosen = jnp.concatenate([jnp.zeros((1, 128), jnp.int32)] + chosen, axis=1)
    chosen = jnp.broadcast_to(chosen, (8, CLUSTERS)).astype(F32).astype(BF16)
    shift = dot(spread, chosen, 1, 1)[:, 0:1].astype(jnp.int32)
    device = octet * 16 + (local + shift) % 16
    spread = onehot(quarter * 128 + device == lane)
    count0 = dot(count0.astype(BF16), spread)
    count1 = dot(count1.astype(BF16), spread)

    at = iota((CLUSTERS, 8), 0)
    upto = iota((CLUSTERS, 8), 1)
    mine = at % 128 == core * CHIPS + chip
    ends_ref[...] = dot(
        count0.astype(BF16), onehot(mine & (at // 128 * 2 <= upto))
    ) + dot(count1.astype(BF16), onehot(mine & (at // 128 * 2 + 1 <= upto)))

    here = iota((CHIPS, CLUSTERS), 0) == chip
    own0 = jnp.sum(jnp.where(here, count0, 0.0), axis=0, keepdims=True)
    own1 = jnp.sum(jnp.where(here, count1, 0.0), axis=0, keepdims=True)
    own = own0 + own1
    start = [jnp.zeros((1, 128), F32)]
    for p in range(3):
        start.append(start[-1] + own[:, p * 128 : (p + 1) * 128])
    start0 = jnp.concatenate(start, axis=1)
    start1 = start0 + own0
    which = iota((8, CLUSTERS), 0)
    device_row = (iota((8, CLUSTERS), 1) % 128).astype(F32)
    table = jnp.where(
        which == 0, device_row, jnp.where(which == 1, start0, jnp.where(which == 2, start1, 0.0))
    ).astype(BF16)
    table = dot(table, spread, 1, 1).astype(BF16)

    def slots(ids, of_core):
        looked = dot(table, onehot(ids[0:1] == iota((CLUSTERS, ROWS), 0)))
        looked = looked.astype(jnp.int32)
        to = looked[0:1]
        k = jnp.where(of_core == 0, looked[1:2], looked[2:3]) + ids[1:2]
        return to, k, jnp.where(to // CHIPS == core, to % CHIPS * CAP + k, -1)

    to, k, slot = slots(ids_ref[...], core)
    _, _, slot2 = slots(ids2_ref[...], 1 - core)
    which = iota((8, ROWS), 0)
    rows_ref[...] = jnp.where(which == 0, to, jnp.where(which == 1, k, 0))
    tile = 256
    for n in range(SLOTS // tile):
        at = iota((tile, ROWS), 0) + n * tile
        out_ref[n * tile : (n + 1) * tile, :] = (
            dot(onehot(slot == at), unit_ref[...]) + dot(onehot(slot2 == at), unit2_ref[...])
        ).astype(BF16)


def pairs_kernel(rows_ref, ends_ref, out_ref):
    ends = ends_ref[...].astype(BF16)

    def keys(at, past):
        chip = at * 2731 // 65536
        k = at - chip * CAP
        n = past(chip, k)
        key = ((chip // 4 * 8 + n % 2 * 4 + chip % 4) * 32) + k
        return n // 2 * 8192, n // 2 * 8192 + key

    def past_col(chip, k):
        ends_col = dot(onehot(chip == iota((SLOTS, CHIPS), 1)), ends)
        return jnp.sum(jnp.where(k.astype(F32) >= ends_col, 1, 0), axis=1, keepdims=True)

    def past_row(chip, k):
        ends_row = dot(ends, onehot(chip == iota((CHIPS, SLOTS), 0)), 0, 0)
        return jnp.sum(jnp.where(k.astype(F32) >= ends_row, 1, 0), axis=0, keepdims=True)

    _, key_col = keys(iota((SLOTS, 1), 0), past_col)
    low_row, key_row = keys(iota((1, SLOTS), 1), past_row)
    tile = 384
    best = []
    for i in range(SLOTS // tile):
        mine = slice(i * tile, (i + 1) * tile)
        top = jnp.full((1, tile), -1.0, F32)
        for j in range(i + 1):
            other = slice(j * tile, (j + 1) * tile)
            score = dot(rows_ref[other, :], rows_ref[mine, :], 1, 1)
            key = key_col[other]
            keep = (key >= low_row[:, mine]) & (key < key_row[:, mine])
            top = jnp.maximum(top, jnp.max(jnp.where(keep, score, -1.0), axis=0, keepdims=True))
        best.append(top)
    best = jnp.concatenate(best, axis=1)
    dev = iota((DEVS, SLOTS), 0)
    chip = iota((1, SLOTS), 1) * 2731 // 65536
    block = jnp.where(dev // 8 * 4 + dev % 4 == chip, best, 0.0)
    at = iota((SLOTS, 128), 0)
    column = jnp.where(at - at * 2731 // 65536 * CAP == iota((SLOTS, 128), 1), 1.0, 0.0)
    out_ref[...] = dot(block, column, precision=lax.Precision.HIGHEST)


def home_kernel(got_ref, rows_ref, out_ref):
    to, k = rows_ref[0:1, :], rows_ref[1:2, :]
    chip = to % CHIPS
    dev = chip // 4 * 8 + to // CHIPS * 4 + chip % 4
    pick = jnp.where(dev == iota((DEVS, ROWS), 0), 1.0, 0.0)
    cand = dot(got_ref[:, 0:32], pick, 0, 0, precision=lax.Precision.HIGHEST)
    best = jnp.sum(jnp.where(k == iota((32, ROWS), 0), cand, 0.0), axis=0, keepdims=True)
    for j in range(ROWS // 128):
        out_ref[j : j + 1, :] = best[:, j * 128 : (j + 1) * 128]


def call(kernel, out_shape, *args, **kwargs):
    return pl.pallas_call(
        kernel,
        out_shape=out_shape,
        compiler_params=pltpu.CompilerParams(vmem_limit_bytes=48 * 2**20),
        **kwargs,
    )(*args)


def shape(*dims, dtype=F32):
    return jax.ShapeDtypeStruct(dims, dtype)


def by_groups(embeddings, owner, local_cluster):
    rows, width = embeddings.shape
    n_groups = GROUPS
    cap = 2 * rows // n_groups
    emb32 = embeddings.astype(F32)
    scale = lax.rsqrt(jnp.mean(emb32 * emb32, axis=1, keepdims=True) + 1e-06) / math.sqrt(width)
    unit = (emb32 * scale).astype(BF16)
    target = owner[:, 0]
    cluster = target * CPG + local_cluster
    device = lax.axis_index(ALL)
    global_id = device * rows + jnp.arange(rows, dtype=jnp.int32)
    onehots = (target[:, None] == jnp.arange(n_groups, dtype=jnp.int32)[None, :]).astype(jnp.int32)
    rank = jnp.sum(jnp.cumsum(onehots, axis=0) * onehots, axis=1) - 1
    slot = target * cap + rank
    size = n_groups * cap

    def send(x, fill):
        full = jnp.full((size,) + x.shape[1:], fill, x.dtype).at[slot].set(x)
        full = full.reshape((n_groups, cap) + x.shape[1:])
        got = lax.all_to_all(full, GROUP_AXES, split_axis=0, concat_axis=0, tiled=True)
        return got.reshape((size,) + x.shape[1:])

    mine, ids, labels = send(unit, 0), send(global_id, -1), send(cluster, -1)
    rows4, ids4, labels4 = (lax.all_gather(x, "x", axis=0, tiled=True) for x in (mine, ids, labels))
    prod = jnp.einsum("id,jd->ij", mine, rows4, preferred_element_type=F32)
    keep = (labels[:, None] == labels4[None, :]) & (ids4[None, :] < ids[:, None])
    best = jnp.maximum(-1.0, jnp.max(jnp.where(keep, prod, -1.0), axis=1))
    back = lax.all_to_all(
        best.reshape(n_groups, cap), GROUP_AXES, split_axis=0, concat_axis=0, tiled=True
    )
    return back.reshape(size)[slot]


def by_devices(packed, ends, places):
    got = lax.all_to_all(
        packed.reshape(CHIPS, CAP, WIDTH), CHIP_AXES, split_axis=0, concat_axis=0, tiled=True
    )
    best = call(pairs_kernel, shape(DEVS, 128), got.reshape(SLOTS, WIDTH), ends)
    back = lax.all_to_all(best, ALL, split_axis=0, concat_axis=0, tiled=True)
    return call(home_kernel, shape(ROWS // 128, 128), back, places).reshape(ROWS)


def body(embeddings, owner, local_cluster):
    hist, ids = call(
        count_kernel,
        (shape(DEVS, 4, 128), shape(8, ROWS, dtype=jnp.int32)),
        owner.reshape(1, ROWS),
        local_cluster.reshape(1, ROWS),
    )
    hists = lax.all_to_all(hist, ALL, split_axis=0, concat_axis=0, tiled=True)
    block = pl.BlockSpec((192, WIDTH), lambda i: (i, 0))
    unit = call(
        unit_kernel,
        shape(ROWS, WIDTH, dtype=BF16),
        embeddings,
        grid=(4,),
        in_specs=[block],
        out_specs=block,
    )
    swap = [(0, 1), (1, 0)]
    unit2, ids2 = lax.ppermute(unit, "core", swap), lax.ppermute(ids, "core", swap)
    packed, ends, places, load = call(
        pack_kernel,
        (
            shape(SLOTS, WIDTH, dtype=BF16),
            shape(CHIPS, 8),
            shape(8, ROWS, dtype=jnp.int32),
            shape(8, 128, dtype=jnp.int32),
        ),
        hists, ids, ids2, unit, unit2,
    )
    return lax.cond(
        load[0, 0] <= CAP,
        lambda: by_devices(packed, ends, places),
        lambda: by_groups(embeddings, owner, local_cluster),
    )


def solution(mesh):
    fine = Mesh(mesh.devices.reshape(4, 4, 2, 4), ALL)
    return jax.shard_map(
        body,
        mesh=fine,
        in_specs=(P(ALL, None), P(ALL, None), P(ALL)),
        out_specs=P(ALL),
        check_vma=False,
    )
```

time: 243 us -> 120 us (0.49)
  waiting for transfers between devices: 83.7 us -> 10.2 us
  matrix products: 24.8 us -> 0 us
  Pallas kernels: 0 us -> 20.4 us
  other arithmetic: 17.6 us -> 0 us
  local copies, waits for them, and re-layouts: 16.7 us -> 1.8 us
  blocking collectives: 69.9 us -> 60.2 us
  starting transfers between devices: 16.1 us -> 12.8 us
    all_gather x1 -> x0, waiting for transfers between devices: 68.2 us -> none  [body(): other_rows = lax.all_gather(mine, 'blk', axis=0, tiled=True)]
    dot_general x1 -> x0, matrix products: 24.8 us -> none  [pair_scores(): jnp.einsum('id,jd->ij', left, right, preferred_element_type=jnp.float32)]
    all_gather x2 -> x0, blocking collectives: 20.8 us -> none  [the longest x1 10.5 us: body(): other_ids = lax.all_gather(ids, 'blk', axis=0, tiled=True)]
    pallas_call x0 -> x5, Pallas kernels: none -> 20.4 us  [call(): pl.pallas_call(kernel, out_shape=out_shape, compiler_params=pltpu.Compile...]
    all_to_all x1 -> x2, blocking collectives: 49.2 us -> 60.2 us  [the longest x1 45.4 us: by_devices(): lax.all_to_all(packed.reshape(CHIPS, CAP, WIDTH), CHIP_AXES, split_axis=0...]
    scatter x1 -> x0, other arithmetic: 10.4 us -> none  [body(): send_rows = jnp.zeros((n_groups * cap, width), jnp.bfloat16).at[slot].set...]
    scatter x2 -> x0, local copies, waits for them, and re-layouts: 6.77 us -> none  [the longest x1 3.38 us: body(): jnp.full((n_groups * cap,), -1, jnp.int32).at[slot].set(global_id)]
    all_to_all x3 -> x1, waiting for transfers between devices: 15.5 us -> 9.36 us  [body(): hists = lax.all_to_all(hist, ALL, split_axis=0, concat_axis=0, tiled=True)]
  transfers between devices with their start and end apart: 4 -> 3, of which waited for: 4 -> 2; matrix products, arithmetic and copies ran while one was open for 4% -> 0% of each run, Pallas kernels for 0% -> 0%
where the time goes in v1:
time: 120 us
  blocking collectives  60.2 us (50%)
  Pallas kernels  20.4 us (17%)
  between operations  14.1 us (12%)
  starting transfers between devices  12.8 us (11%)
  waiting for transfers between devices  10.2 us (8%)
  local copies, waits for them, and re-layouts  1.8 us (2%)
    all_to_all x1, blocking collectives, by_devices(): lax.all_to_all(packed.reshape(CHIPS, CAP, WIDTH), CHIP_AXES, split_axis=0...  45.4 us
    pallas_call x5, Pallas kernels, call(): pl.pallas_call(kernel, out_shape=out_shape, compiler_params=pltpu.Compile...  20.4 us
    all_to_all x1, blocking collectives, by_devices(): back = lax.all_to_all(best, ALL, split_axis=0, concat_axis=0, tiled=True)  14.8 us
    all_to_all x1, starting transfers between devices, body(): hists = lax.all_to_all(hist, ALL, split_axis=0, concat_axis=0, tiled=True)  10.2 us
    all_to_all x1, waiting for transfers between devices, body(): hists = lax.all_to_all(hist, ALL, split_axis=0, concat_axis=0, tiled=True)  9.36 us
  transfers between devices with their start and end apart: 3, of which 2 were waited for; matrix products, arithmetic and copies ran while one was open for 0% of the time, Pallas kernels for 0%

profile of v1, /device:TPU:1, one launch (start us, length us, event | category | flops | bytes accessed | tf_op | source)
XLA Modules:
  0.0 119.8 jit_solution(1706991796517955729)
XLA Ops:
  6.5 0.0 copy-start.4
  6.5 0.0 copy-start.3
  6.5 2.6 %shard_map.40.unit_ref = bf16[768,1024]{1,0:T(8,128)(2,1)S(1)} custom-call(bf16[768,1024]{1,0:T(8,128)(2,1)} %emb_ref.1), custom_call_target="tpu_custom_call" | custom-call | tf_op jit(solution)/shard_map/pallas_call | solution.py:236
  9.1 1.5 %collective-permute-start.1 = (bf16[768,1024]{1,0:T(8,128)(2,1)S(1)}, bf16[768,1024]{1,0:T(8,128)(2,1)S(1)}, u32[]{:S(2)}, u32[]{:S(2)}) collective-permute-start(bf16[768,1024]{1,0:T(8,128)(2,1)S(1)} %shard_map.40.unit_ref), channel_id=1, source_target_pairs={{0,4},{4,0},{1,5},{5,1},{2,6},{6,2},{3,7},{7,3},{8,12},{12,8},{9,1... | collective-permute-start | bytes 4718600 | tf_op jit(solution)/shard_map/ppermute | solution.py:308
  10.6 0.0 copy-done.4
  10.6 0.0 copy-done.3
  10.6 0.5 shard_map.39
  11.1 0.0 copy-start
  11.1 0.7 copy-done
  11.8 10.2 %all-to-all-start.6 = ((f32[128,4,128]{2,1,0:T(4,128)}), f32[128,4,128]{2,1,0:T(4,128)S(1)}, u32[]{:S(2)}, u32[]{:S(2)}) async-start(f32[128,4,128]{2,1,0:T(4,128)} %copy-done), calls=%async_computation.6 | async-start | bytes 524288 | tf_op jit(solution)/shard_map/all_to_all | solution.py:297
  22.0 1.1 collective-permute-start
  23.2 0.8 collective-permute-done.ids2_ref
  24.0 9.4 %all-to-all-done.6.hist_ref = f32[128,4,128]{2,1,0:T(4,128)S(1)} async-done(((f32[128,4,128]{2,1,0:T(4,128)}), f32[128,4,128]{2,1,0:T(4,128)S(1)}, u32[]{:S(2)}, u32[]{:S(2)}) %all-to-all-start.6) | async-done | bytes 262176 | tf_op jit(solution)/shard_map/all_to_all | solution.py:297
  33.4 0.0 collective-permute-done.1.unit2_ref
  33.4 10.5 %shard_map.41 = (bf16[1536,1024]{1,0:T(8,128)(2,1)}, f32[64,8]{1,0:T(8,128)S(1)}, s32[8,768]{1,0:T(8,128)S(1)}, s32[8,128]{1,0:T(8,128)S(1)}) custom-call(f32[128,4,128]{2,1,0:T(4,128)S(1)} %all-to-all-done.6.hist_ref, s32[8,768]{1,0:T(8,128)S(1)} %get-tuple-element.33.ids_ref, s32[8,768]{1,0:T(8,128)S(1)} %collective-permute-done.ids2_ref, ...), custom_call_target="tpu_custom_call" | custom-call | tf_op jit(solution)/shard_map/pallas_call | solution.py:236
  43.8 0.5 slice.9
  45.0 67.4 %conditional.1 = (f32[768]{0:T(1024)S(1)}) conditional(s32[]{:T(128)} %bitcast.12, (s32[768,1]{0,1:T(1,128)S(1)}, s32[768]{0:T(1024)S(1)}, bf16[768,1024]{1,0:T(8,128)(2,1)}) %tuple.20, (bf16[1536,1024]{1,0:T(8,128)(2,1)}, f32[64,8]{1,0:T(8,128)S(1)}, s32[8,768]{1,0:T(8,128)S(1)}) %tuple.12), branch_computations={%region_0.9_spmd, %region_9.10_spmd} | conditional | flops 19382534144 | bytes 95247704 | solution.py:319
  45.3 45.4 %all_to_all.41 = bf16[64,24,1024]{2,1,0:T(8,128)(2,1)S(1)} all-to-all(bf16[64,24,1024]{2,1,0:T(8,128)(2,1)} %bitcast.40), channel_id=1, replica_groups=mesh['z'=4,'y'=4,'core'=2,'x'=4] {'z','y','x'}, dimensions={0} | all-to-all | bytes 6291456 | tf_op jit(solution)/shard_map/cond/branch_1_fun/all_to_all | solution.py:282
  90.7 6.5 %branch_1_fun.2 = f32[128,128]{1,0:T(8,128)S(1)} custom-call(bf16[1536,1024]{1,0:T(8,128)(2,1)S(1)} %bitcast.34, f32[64,8]{1,0:T(8,128)S(1)} %get-tuple-element.24.ends_ref), custom_call_target="tpu_custom_call" | custom-call | tf_op jit(solution)/shard_map/cond/branch_1_fun/pallas_call | solution.py:236
  97.2 14.8 %all_to_all.42 = f32[128,1,128]{2,1,0:T(1,128)S(1)} all-to-all(f32[128,1,128]{2,1,0:T(1,128)S(1)} %bitcast.35), channel_id=1, replica_groups=mesh['z'=4,'y'=4,'core'=2,'x'=4] {'z','y','core','x'}, dimensions={0} | all-to-all | bytes 131072 | tf_op jit(solution)/shard_map/cond/branch_1_fun/all_to_all | solution.py:286
  112.0 0.4 branch_1_fun.3
  112.4 0.0 copy-start.5
  112.4 0.6 copy-done.5
  (1 shorter events, 0.0 us)
Async XLA Ops:
  6.5 4.1 %copy-start.4 = (s32[768]{0:T(1024)S(1)}, s32[768]{0:T(1024)}, u32[]{:S(2)}) copy-start(s32[768]{0:T(1024)} %param.7) | copy-start | bytes 9220
  6.5 4.1 %copy-start.3 = (s32[768,1]{0,1:T(1,128)S(1)}, s32[768,1]{0,1:T(1,128)}, u32[]{:S(2)}) copy-start(s32[768,1]{0,1:T(1,128)} %param.6) | copy-start | bytes 9220
  9.1 24.2 %collective-permute-start.1 = (bf16[768,1024]{1,0:T(8,128)(2,1)S(1)}, bf16[768,1024]{1,0:T(8,128)(2,1)S(1)}, u32[]{:S(2)}, u32[]{:S(2)}) collective-permute-start(bf16[768,1024]{1,0:T(8,128)(2,1)S(1)} %shard_map.40.unit_ref), channel_id=1, source_target_pairs={{0,4},{4,0},{1,5},{5,1},{2,6},{6,2},{3,7},{7,3},{8,12},{12,8},{9,1... | collective-permute-start | bytes 4718600 | tf_op jit(solution)/shard_map/ppermute | solution.py:308
  11.1 0.7 copy-start
  11.8 21.6 %all-to-all-start.6 = ((f32[128,4,128]{2,1,0:T(4,128)}), f32[128,4,128]{2,1,0:T(4,128)S(1)}, u32[]{:S(2)}, u32[]{:S(2)}) async-start(f32[128,4,128]{2,1,0:T(4,128)} %copy-done), calls=%async_computation.6 | async-start | bytes 524288 | tf_op jit(solution)/shard_map/all_to_all | solution.py:297
  22.0 2.0 %collective-permute-start = (s32[8,768]{1,0:T(8,128)S(1)}, s32[8,768]{1,0:T(8,128)S(1)}, u32[]{:S(2)}, u32[]{:S(2)}) collective-permute-start(s32[8,768]{1,0:T(8,128)S(1)} %get-tuple-element.33.ids_ref), channel_id=1, source_target_pairs={{0,4},{4,0},{1,5},{5,1},{2,6},{6,2},{3,7},{7,3},{8,12},{12,8},{9,1... | collective-permute-start | bytes 73736 | tf_op jit(solution)/shard_map/ppermute | solution.py:308
  112.4 0.6 copy-start.5

commit v2 on v1

v2 whole, which is shorter than its diff:
```python
import itertools
import math

import jax
import jax.numpy as jnp
from jax import lax
from jax.experimental import pallas as pl
from jax.experimental.pallas import tpu as pltpu
from jax.sharding import Mesh, PartitionSpec as P

CPG = 16
GROUPS = 32
CLUSTERS = GROUPS * CPG
ROWS = 768
WIDTH = 1024
CHIPS = 64
DEVS = 128
CAP = 24
SLOTS = CHIPS * CAP
TILE = 384
HELD = 896
ALL = ("z", "y", "core", "x")
GROUP_AXES = ("z", "y", "core")
CHIP_AXES = ("z", "y", "x")
ORDERS = tuple(itertools.permutations(range(4)))
BF16 = jnp.bfloat16
ANY = pl.BlockSpec(memory_space=pl.ANY)
HBM = pl.BlockSpec(memory_space=pltpu.HBM)
F32 = jnp.float32


def iota(shape, dim):
    return lax.broadcasted_iota(jnp.int32, shape, dim)


def dot(a, b, ca=1, cb=0, precision=None):
    return lax.dot_general(
        a, b, (((ca,), (cb,)), ((), ())), preferred_element_type=F32, precision=precision
    )


def onehot(cond):
    return jnp.where(cond, 1.0, 0.0).astype(BF16)


def place():
    zy = lax.axis_index("z") * 4 + lax.axis_index("y")
    return lax.axis_index("core"), zy * 4 + lax.axis_index("x")


def count_kernel(owner_ref, local_ref, hist_ref, ids_ref, hists, sem):
    owner = owner_ref[...]
    local = jnp.concatenate([local_ref[j : j + 1, :] for j in range(ROWS // 128)], axis=1)
    by_owner = onehot(owner == iota((GROUPS, ROWS), 0))
    by_local = onehot(local == iota((CPG, ROWS), 0))
    pairs = dot(by_owner, by_local, 1, 1).astype(BF16)
    spread = onehot(iota((CPG, CLUSTERS), 1) % CPG == iota((CPG, CLUSTERS), 0))
    wide = dot(pairs, spread)
    mine = iota((GROUPS, CLUSTERS), 1) // CPG == iota((GROUPS, CLUSTERS), 0)
    counts = jnp.sum(jnp.where(mine, wide, 0.0), axis=0, keepdims=True)
    for j in range(CLUSTERS // 128):
        part = counts[:, j * 128 : (j + 1) * 128]
        hists[:, j, :] = jnp.broadcast_to(part, (DEVS, 128))
    leave = pltpu.make_async_copy(hists, hist_ref, sem)
    leave.start()
    cluster = owner * CPG + local
    eye = iota((128, 128), 0) == iota((128, 128), 1)
    rank = jnp.zeros((1, ROWS), jnp.int32)
    for j in range(ROWS // 128):
        part = jnp.broadcast_to(cluster[:, j * 128 : (j + 1) * 128], (128, 128))
        column = jnp.sum(jnp.where(eye, part, 0), axis=1, keepdims=True)
        width = ROWS - j * 128
        later = iota((128, width), 1) > iota((128, width), 0)
        hit = jnp.where((column == cluster[:, j * 128 :]) & later, 1, 0)
        found = jnp.sum(hit, axis=0, keepdims=True)
        if j:
            found = jnp.concatenate([jnp.zeros((1, j * 128), jnp.int32), found], axis=1)
        rank = rank + found
    which = iota((8, ROWS), 0)
    ids_ref[...] = jnp.where(which == 0, cluster, jnp.where(which == 1, rank, 0))
    leave.wait()


def wide_row(row):
    return jnp.broadcast_to(row.astype(F32), (8, row.shape[1])).astype(BF16)


def parity(cluster):
    return cluster & 1


def before(flags):
    tri = onehot(iota((256, 256), 0) < iota((256, 256), 1))
    seen, parts = jnp.zeros((1, 1), F32), []
    for j in range(ROWS // 256):
        part = flags[:, j * 256 : (j + 1) * 256]
        parts.append(dot(wide_row(part), tri)[0:1] + seen)
        seen = seen + jnp.sum(part, axis=1, keepdims=True)
    return jnp.concatenate(parts, axis=1), seen


def gather_kernel(ids_ref, ids2_ref, emb_ref, emb2_ref, out_ref, ids_out_ref, raw, raw2, sems):
    core, _ = place()
    reads = [
        pltpu.make_async_copy(emb_ref, raw, sems.at[0]),
        pltpu.make_async_copy(emb2_ref, raw2, sems.at[1]),
    ]
    for read in reads:
        read.start()
    ids, ids2 = ids_ref[...], ids2_ref[...]
    flags, flags2 = (jnp.where(parity(i[0:1]) == core, 1.0, 0.0) for i in (ids, ids2))
    slot, total = before(flags)
    slot2, _ = before(flags2)
    slot = jnp.where(flags > 0, slot, -1.0)
    slot2 = jnp.where(flags2 > 0, slot2 + total, -1.0)
    tile = 256
    at = iota((tile, ROWS), 0).astype(F32).astype(BF16)
    owner_of = [
        jnp.concatenate(
            [(i[0:1] >> 4).astype(F32), (i[0:1] & 15).astype(F32), i[1:2].astype(F32), jnp.full((1, ROWS), 1.0 + n)]
            + [jnp.zeros((4, ROWS), F32)],
            axis=0,
        ).astype(BF16)
        for n, i in enumerate((ids, ids2))
    ]
    for read in reads:
        read.wait()
    for low in range(0, HELD, tile):
        high = min(low + tile, HELD)
        picks = [
            jnp.where(jnp.clip(s - low, -1, tile).astype(BF16) == at[: high - low], BF16(1), BF16(0))
            for s in (slot, slot2)
        ]
        out_ref[low:high, :] = (dot(picks[0], raw[...]) + dot(picks[1], raw2[...])).astype(BF16)
        ids_out_ref[:, low:high] = (
            dot(owner_of[0], picks[0], 1, 1) + dot(owner_of[1], picks[1], 1, 1)
        ).astype(jnp.int32)


def rotate(value, by, run=16):
    if by == 0:
        return value
    inside = (iota(value.shape, 1) & (run - 1)) >= by
    return jnp.where(inside, pltpu.roll(value, by, 1), pltpu.roll(value, by + 128 - run, 1))


def settle(base, parts):
    turned = [[rotate(part, r, 4) for r in range(4)] for part in parts]
    tops = [
        jnp.concatenate([jnp.max(base + t[r], axis=0, keepdims=True) for t in turned], axis=0)
        for r in range(4)
    ]
    lane4 = iota(tops[0].shape, 1) & 3
    best = turn = None
    for order in ORDERS:
        turns = [(j - order[j]) & 3 for j in range(4)]
        load, spin = tops[turns[3]], jnp.full(tops[0].shape, turns[3], jnp.int32)
        for j in range(3):
            load = jnp.where(lane4 == j, tops[turns[j]], load)
            spin = jnp.where(lane4 == j, turns[j], spin)
        load = jnp.maximum(load, rotate(load, 1, 4))
        load = jnp.maximum(load, rotate(load, 2, 4))
        if best is None:
            best, turn = load, spin
        else:
            turn = jnp.where(load < best, spin, turn)
            best = jnp.minimum(load, best)
    return best, turn, turned


def placing(parts):
    lane = iota((1, 128), 1)
    base, sources = parts[0], [lane]
    for part in parts[1:3]:
        _, turn, (turned,) = settle(base, [part])
        chosen = turned[0]
        for r in range(1, 4):
            chosen = jnp.where(turn == r, turned[r], chosen)
        base = base + chosen
        sources.append((lane & ~3) | ((lane - turn) & 3))
    loads, turns, _ = settle(base, [rotate(parts[3], 2 * c, 8) for c in range(4)])
    loads = jnp.maximum(loads, rotate(loads, 4, 8))
    best, turn, by = loads[0:1], turns[0:1], jnp.zeros((1, 128), jnp.int32)
    for c in range(1, 4):
        better = loads[c : c + 1] < best
        best = jnp.where(better, loads[c : c + 1], best)
        turn = jnp.where(better, turns[c : c + 1], turn)
        by = jnp.where(better, 2 * c, by)
    run = (lane & ~3) | ((lane - turn) & 3)
    sources.append((lane & ~7) | ((run - by) & 7))
    return jnp.max(best, axis=1, keepdims=True), sources


def column(weights, rows):
    rows = [row.astype(F32) for row in rows]
    rows = jnp.concatenate(rows + [jnp.zeros((8 - len(rows), rows[0].shape[1]), F32)], axis=0)
    which = iota((8, 128), 0)
    weight = jnp.zeros((8, 128), F32)
    for n, w in enumerate(weights):
        weight = jnp.where(which == n, float(w), weight)
    return dot(rows.astype(BF16), weight.astype(BF16), 0, 0)


def same(col, row):
    parts = [onehot(col == row[:, j * 128 : (j + 1) * 128]) for j in range(row.shape[1] // 128)]
    return jnp.concatenate(parts, axis=1)


def place_kernel(
    hist_ref, ids_ref, held_ref, raw_ref, out_ref, ends_ref, rows_ref, load_ref
):
    core, chip = place()
    hist = jnp.concatenate([hist_ref[:, j, :] for j in range(4)], axis=1).astype(BF16)
    dev = iota((CHIPS, DEVS), 1)
    first = (iota((CHIPS, DEVS), 0) >> 2) * 8 + (iota((CHIPS, DEVS), 0) & 3)
    count0 = dot(onehot(dev == first), hist)
    count1 = dot(onehot(dev == first + 4), hist)
    both = (count0 + count1).astype(BF16)

    in_group = onehot((iota((GROUPS, CLUSTERS), 1) >> 4) == iota((GROUPS, CLUSTERS), 0))
    size_row = jnp.sum(dot(both, in_group, 1, 1), axis=0, keepdims=True)
    size_col = jnp.sum(dot(in_group, both, 1, 1), axis=1, keepdims=True)
    lower = iota((GROUPS, GROUPS), 0) < iota((GROUPS, GROUPS), 1)
    ahead = (size_col > size_row) | ((size_col == size_row) & lower)
    order = jnp.sum(jnp.where(ahead, 1.0, 0.0), axis=0, keepdims=True)
    order = dot(wide_row(order), in_group)[0:1].astype(jnp.int32)
    quarter = jnp.where(order < 16, order >> 3, 3 - (order & 1))
    octet = jnp.where(order < 8, order, jnp.where(order < 16, 15 - order, (31 - order) >> 1))
    local = iota((1, CLUSTERS), 1) & 15
    where = column((128, 16, 8, 1), (quarter, octet, local & 1, local >> 1))

    wide = dot(both, same(where, iota((1, CLUSTERS), 1).astype(F32)))
    load, sources = placing([wide[:, p * 128 : (p + 1) * 128] for p in range(4)])
    odd = onehot(parity(iota((CLUSTERS, 128), 0)) == 1)
    of_odd = dot(both, odd)
    of_all = jnp.sum(both.astype(F32), axis=1, keepdims=True)
    held = jnp.max(jnp.maximum(of_odd, of_all - of_odd), axis=0, keepdims=True)[:, 0:1]
    load_ref[...] = jnp.where(held <= HELD, load, 2.0 * CAP).astype(jnp.int32)
    sources = [source + p * 128 for p, source in enumerate(sources)]
    spread = same(where, jnp.concatenate(sources, axis=1).astype(F32))
    count0 = dot(count0.astype(BF16), spread)
    count1 = dot(count1.astype(BF16), spread)

    at = iota((CLUSTERS, 8), 0)
    upto = iota((CLUSTERS, 8), 1)
    mine = (at & 127) == (chip >> 3) * 16 + core * 8 + (chip & 7)
    ends_ref[...] = dot(
        count0.astype(BF16), onehot(mine & ((at >> 7) * 2 <= upto))
    ) + dot(count1.astype(BF16), onehot(mine & ((at >> 7) * 2 + 1 <= upto)))

    here = iota((CHIPS, CLUSTERS), 0) == chip
    own0 = jnp.sum(jnp.where(here, count0, 0.0), axis=0, keepdims=True)
    own1 = jnp.sum(jnp.where(here, count1, 0.0), axis=0, keepdims=True)
    own = own0 + own1
    start = [jnp.zeros((1, 128), F32)]
    for p in range(3):
        start.append(start[-1] + own[:, p * 128 : (p + 1) * 128])
    start0 = jnp.concatenate(start, axis=1)
    start1 = start0 + own0
    device_row = (iota((1, CLUSTERS), 1) & 127).astype(F32)
    by_group = dot(in_group, spread)
    by_local = onehot((iota((CPG, CLUSTERS), 1) & 15) == iota((CPG, CLUSTERS), 0))
    by_local = dot(by_local, spread).astype(BF16)

    def table(row):
        return dot(by_local, (by_group * row).astype(BF16), 1, 1).astype(BF16)

    to_table, table0, table1 = table(device_row), table(start0), table(start1)

    def slots(group, local, rank, start, rows):
        group = onehot(group == iota((GROUPS, rows), 0))
        local = local == iota((CPG, rows), 0)

        def look(table):
            return jnp.sum(jnp.where(local, dot(table, group), 0.0), axis=0, keepdims=True).astype(jnp.int32)

        return look(to_table), look(start) + rank

    ids = ids_ref[...]
    first = jnp.where(core == 0, table0, table1)
    to, k = slots(ids[0:1] >> 4, ids[0:1] & 15, ids[1:2], first, ROWS)
    rows_ref[...] = jnp.concatenate([to, k, jnp.zeros((6, ROWS), jnp.int32)], axis=0)
    held = held_ref[...]
    group, local, rank, whose = (held[n : n + 1] for n in range(4))
    to, k = slots(group, local, rank, first, HELD)
    _, k2 = slots(group, local, rank, jnp.where(core == 0, table1, table0), HELD)
    k = jnp.where(whose == 1, k, k2)
    slot = jnp.where(whose > 0, ((to >> 4) * 8 + (to & 7)) * CAP + k, -1)
    tile = 256
    at = iota((tile, HELD), 0).astype(F32).astype(BF16)
    for n in range(SLOTS // tile):
        pick = jnp.clip(slot - n * tile, -1, tile).astype(F32).astype(BF16)
        rows = dot(jnp.where(pick == at, BF16(1), BF16(0)), raw_ref[...])
        scale = lax.rsqrt(jnp.mean(rows * rows, axis=1, keepdims=True) + 1e-06) / math.sqrt(WIDTH)
        out_ref[n * tile : (n + 1) * tile, :] = (rows * scale).astype(BF16)


def pairs_kernel(rows_ref, ends_ref, out_ref):
    at = iota((1, SLOTS), 1)
    chip = at * 2731 >> 16
    k = at - chip * CAP
    own_chip = chip == iota((CHIPS, SLOTS), 0)
    ends = dot(ends_ref[...].astype(BF16), onehot(own_chip), 0, 0)
    past = jnp.sum(jnp.where(k.astype(F32) >= ends, 1, 0), axis=0, keepdims=True)
    label = past >> 1
    dev = (chip >> 2) * 8 + (past & 1) * 4 + (chip & 3)
    label_col = column((1,), (label,))
    order_col = column((32, 1), (dev, k))
    label_row = label.astype(F32)
    order_row = (dev * 32 + k).astype(F32)
    best = []
    for i in range(SLOTS // TILE):
        mine = slice(i * TILE, (i + 1) * TILE)
        top = jnp.full((1, TILE), -1.0, F32)
        for j in range(i + 1):
            other = slice(j * TILE, (j + 1) * TILE)
            score = dot(rows_ref[other, :], rows_ref[mine, :], 1, 1)
            tops = []
            for c in range(TILE // 128):
                part = slice(i * TILE + c * 128, i * TILE + (c + 1) * 128)
                keep = label_col[other] == label_row[:, part]
                if i == j:
                    keep = keep & (order_col[other] < order_row[:, part])
                part = jnp.where(keep, score[:, c * 128 : (c + 1) * 128], -1.0)
                tops.append(jnp.max(part, axis=0, keepdims=True))
            top = jnp.maximum(top, jnp.concatenate(tops, axis=1))
        best.append(top)
    best = jnp.concatenate(best, axis=1)
    block = jnp.where(own_chip, best, 0.0)
    at = iota((SLOTS, 128), 0)
    place_col = jnp.where(at - (at * 2731 >> 16) * CAP == iota((SLOTS, 128), 1), 1.0, 0.0)
    found = dot(block, place_col, precision=lax.Precision.HIGHEST)
    for n in range(DEVS // 8):
        four = found[n * 4 : (n + 1) * 4, :]
        out_ref[n * 8 : (n + 1) * 8, :] = jnp.concatenate([four, four], axis=0)


def home_kernel(got_ref, rows_ref, out_ref):
    to, k = rows_ref[0:1, :], rows_ref[1:2, :]
    chip = (to >> 4) * 8 + (to & 7)
    dev = (chip >> 2) * 8 + ((to >> 3) & 1) * 4 + (chip & 3)
    pick = jnp.where(dev == iota((DEVS, ROWS), 0), 1.0, 0.0)
    cand = dot(got_ref[:, 0:32], pick, 0, 0, precision=lax.Precision.HIGHEST)
    best = jnp.sum(jnp.where(k == iota((32, ROWS), 0), cand, 0.0), axis=0, keepdims=True)
    for j in range(ROWS // 128):
        out_ref[j : j + 1, :] = best[:, j * 128 : (j + 1) * 128]


def call(kernel, out_shape, *args, vmem=32 * 2**20, **kwargs):
    return pl.pallas_call(
        kernel,
        out_shape=out_shape,
        compiler_params=pltpu.CompilerParams(vmem_limit_bytes=vmem),
        **kwargs,
    )(*args)


def shape(*dims, dtype=F32):
    return jax.ShapeDtypeStruct(dims, dtype)


def by_groups(embeddings, owner, local_cluster):
    rows, width = embeddings.shape
    n_groups = GROUPS
    cap = 2 * rows // n_groups
    emb32 = embeddings.astype(F32)
    scale = lax.rsqrt(jnp.mean(emb32 * emb32, axis=1, keepdims=True) + 1e-06) / math.sqrt(width)
    unit = (emb32 * scale).astype(BF16)
    target = owner[:, 0]
    cluster = target * CPG + local_cluster
    device = lax.axis_index(ALL)
    global_id = device * rows + jnp.arange(rows, dtype=jnp.int32)
    onehots = (target[:, None] == jnp.arange(n_groups, dtype=jnp.int32)[None, :]).astype(jnp.int32)
    rank = jnp.sum(jnp.cumsum(onehots, axis=0) * onehots, axis=1) - 1
    slot = target * cap + rank
    size = n_groups * cap

    def send(x, fill):
        full = jnp.full((size,) + x.shape[1:], fill, x.dtype).at[slot].set(x)
        full = full.reshape((n_groups, cap) + x.shape[1:])
        got = lax.all_to_all(full, GROUP_AXES, split_axis=0, concat_axis=0, tiled=True)
        return got.reshape((size,) + x.shape[1:])

    mine, ids, labels = send(unit, 0), send(global_id, -1), send(cluster, -1)
    rows4, ids4, labels4 = (lax.all_gather(x, "x", axis=0, tiled=True) for x in (mine, ids, labels))
    prod = jnp.einsum("id,jd->ij", mine, rows4, preferred_element_type=F32)
    keep = (labels[:, None] == labels4[None, :]) & (ids4[None, :] < ids[:, None])
    best = jnp.maximum(-1.0, jnp.max(jnp.where(keep, prod, -1.0), axis=1))
    back = lax.all_to_all(
        best.reshape(n_groups, cap), GROUP_AXES, split_axis=0, concat_axis=0, tiled=True
    )
    return back.reshape(size)[slot]


def by_devices(packed, ends):
    blocks = packed.reshape(CHIPS, CAP, WIDTH)
    got = lax.all_to_all(blocks, CHIP_AXES, split_axis=0, concat_axis=0, tiled=True)
    best = call(
        pairs_kernel, shape(DEVS, 128), got.reshape(SLOTS, WIDTH), ends
    )
    return best


def body(embeddings, owner, local_cluster):
    hist, ids = call(
        count_kernel,
        (shape(DEVS, 4, 128), shape(8, ROWS, dtype=jnp.int32)),
        owner.reshape(1, ROWS),
        local_cluster.reshape(ROWS // 128, 128),
        out_specs=(HBM, pl.BlockSpec()),
        scratch_shapes=[pltpu.VMEM((DEVS, 4, 128), F32), pltpu.SemaphoreType.DMA],
    )
    swap = [(0, 1), (1, 0)]
    ids2 = lax.ppermute(ids, "core", swap)
    hists = lax.all_to_all(hist, ALL, split_axis=0, concat_axis=0, tiled=True)
    embeddings2 = lax.ppermute(embeddings, "core", swap)
    raw, held = call(
        gather_kernel,
        (shape(HELD, WIDTH, dtype=BF16), shape(8, HELD, dtype=jnp.int32)),
        ids, ids2, embeddings, embeddings2,
        in_specs=[pl.BlockSpec()] * 2 + [ANY] * 2,
        scratch_shapes=[
            pltpu.VMEM((ROWS, WIDTH), BF16),
            pltpu.VMEM((ROWS, WIDTH), BF16),
            pltpu.SemaphoreType.DMA((2,)),
        ],
    )
    packed, ends, places, load = call(
        place_kernel,
        (
            shape(SLOTS, WIDTH, dtype=BF16),
            shape(CHIPS, 8),
            shape(8, ROWS, dtype=jnp.int32),
            shape(1, 1, dtype=jnp.int32),
        ),
        hists, ids, held, raw,
    )
    best = by_devices(packed, ends)
    back = lax.all_to_all(best, ALL, split_axis=0, concat_axis=0, tiled=True)
    return lax.cond(
        load.reshape(()) <= CAP,
        lambda: call(home_kernel, shape(ROWS // 128, 128), back, places).reshape(ROWS),
        lambda: by_groups(embeddings, owner, local_cluster),
    )


def solution(mesh):
    fine = Mesh(mesh.devices.reshape(4, 4, 2, 4), ALL)
    return jax.shard_map(
        body,
        mesh=fine,
        in_specs=(P(ALL, None), P(ALL, None), P(ALL)),
        out_specs=P(ALL),
        check_vma=False,
    )
```

time: 120 us -> 115 us (0.958)
  blocking collectives: 60.2 us -> 46.3 us
  starting transfers between devices: 12.8 us -> 18.7 us
  waiting for transfers between devices: 10.2 us -> 13.7 us
  local copies, waits for them, and re-layouts: 1.8 us -> 0.6 us
    all_to_all x2 -> x1, blocking collectives: 60.2 us -> 46.3 us  [by_devices(): lax.all_to_all(blocks, CHIP_AXES, split_axis=0, concat_axis=0, tiled=True)]
    all_to_all x0 -> x1, waiting for transfers between devices: none -> 9.04 us  [body(): back = lax.all_to_all(best, ALL, split_axis=0, concat_axis=0, tiled=True)]
    all_to_all x1, waiting for transfers between devices: 9.36 us -> 3.82 us  [body(): hists = lax.all_to_all(hist, ALL, split_axis=0, concat_axis=0, tiled=True)]
    all_to_all x0 -> x1, starting transfers between devices: none -> 5.44 us  [body(): back = lax.all_to_all(best, ALL, split_axis=0, concat_axis=0, tiled=True)]
  transfers between devices with their start and end apart: 3 -> 4, of which waited for: 2 -> 3; matrix products, arithmetic and copies ran while one was open for 0% -> 0% of each run, Pallas kernels for 0% -> 6%
where the time goes in v2:
time: 115 us; the launch traced here: 114 us
  blocking collectives  46.3 us (40%)
  Pallas kernels  20.8 us (18%)
  starting transfers between devices  18.7 us (16%)
  between operations  14.1 us (12%)
  waiting for transfers between devices  13.7 us (12%)
    all_to_all x1, blocking collectives, by_devices(): lax.all_to_all(blocks, CHIP_AXES, split_axis=0, concat_axis=0, tiled=True)  46.3 us
    pallas_call x5, Pallas kernels, call(): pl.pallas_call(kernel, out_shape=out_shape, compiler_params=pltpu.Compile...  20.8 us
    all_to_all x1, starting transfers between devices, body(): hists = lax.all_to_all(hist, ALL, split_axis=0, concat_axis=0, tiled=True)  10.7 us
    all_to_all x1, waiting for transfers between devices, body(): back = lax.all_to_all(best, ALL, split_axis=0, concat_axis=0, tiled=True)  9.04 us
    all_to_all x1, starting transfers between devices, body(): back = lax.all_to_all(best, ALL, split_axis=0, concat_axis=0, tiled=True)  5.44 us
    all_to_all x1, waiting for transfers between devices, body(): hists = lax.all_to_all(hist, ALL, split_axis=0, concat_axis=0, tiled=True)  3.82 us
  transfers between devices with their start and end apart: 4, of which 3 were waited for; matrix products, arithmetic and copies ran while one was open for 0% of the time, Pallas kernels for 6%

profile of v2, /device:TPU:1, one launch (start us, length us, event | category | flops | bytes accessed | tf_op | source)
XLA Modules:
  0.0 114.2 jit_solution(9590759449669247649)
XLA Ops:
  6.5 1.4 %collective-permute-start.1 = (bf16[768,1024]{1,0:T(8,128)(2,1)}, bf16[768,1024]{1,0:T(8,128)(2,1)S(1)}, u32[]{:S(2)}, u32[]{:S(2)}) collective-permute-start(bf16[768,1024]{1,0:T(8,128)(2,1)} %emb_ref.1), channel_id=1, source_target_pairs={{0,4},{4,0},{1,5},{5,1},{2,6},{6,2},{3,7},{7,3},{8,12},{12,8},{9,1... | collective-permute-start | bytes 4718600 | tf_op jit(solution)/shard_map/ppermute | solution.py:416
  8.0 1.9 %shard_map.39 = (f32[128,4,128]{2,1,0:T(4,128)}, s32[8,768]{1,0:T(8,128)S(1)}) custom-call(s32[1,768]{1,0:T(1,128)} %bitcast.45, s32[6,128]{1,0:T(8,128)} %bitcast.49), custom_call_target="tpu_custom_call" | custom-call | tf_op jit(solution)/shard_map/pallas_call | solution.py:350
  9.8 10.7 %all-to-all-start.4 = ((f32[128,4,128]{2,1,0:T(4,128)}), f32[128,4,128]{2,1,0:T(4,128)}, u32[]{:S(2)}, u32[]{:S(2)}) async-start(f32[128,4,128]{2,1,0:T(4,128)} %get-tuple-element.32), calls=%async_computation.4 | async-start | bytes 524288 | tf_op jit(solution)/shard_map/all_to_all | solution.py:415
  20.5 1.2 %collective-permute-start = (s32[8,768]{1,0:T(8,128)S(1)}, s32[8,768]{1,0:T(8,128)S(1)}, u32[]{:S(2)}, u32[]{:S(2)}) collective-permute-start(s32[8,768]{1,0:T(8,128)S(1)} %get-tuple-element.33.ids_ref), channel_id=1, source_target_pairs={{0,4},{4,0},{1,5},{5,1},{2,6},{6,2},{3,7},{7,3},{8,12},{12,8},{9,1... | collective-permute-start | bytes 73736 | tf_op jit(solution)/shard_map/ppermute | solution.py:414
  21.7 0.8 collective-permute-done.ids2_ref
  22.6 0.0 collective-permute-done.1.emb2_ref
  22.6 5.1 %shard_map.40 = (bf16[896,1024]{1,0:T(8,128)(2,1)S(1)}, s32[8,896]{1,0:T(8,128)S(1)}) custom-call(s32[8,768]{1,0:T(8,128)S(1)} %get-tuple-element.33.ids_ref, s32[8,768]{1,0:T(8,128)S(1)} %collective-permute-done.ids2_ref, bf16[768,1024]{1,0:T(8,128)(2,1)} %emb_ref.1, bf16[768,1024]{1,0:T(8,128)(2,1)S(1)} %collective-permute-done.1.emb2_ref), custom_call_target="tpu_custom_call" | custom-call | tf_op jit(solution)/shard_map/pallas_call | solution.py:350
  27.7 3.8 %all-to-all-done.4.hist_ref = f32[128,4,128]{2,1,0:T(4,128)} async-done(((f32[128,4,128]{2,1,0:T(4,128)}), f32[128,4,128]{2,1,0:T(4,128)}, u32[]{:S(2)}, u32[]{:S(2)}) %all-to-all-start.4) | async-done | bytes 262176 | tf_op jit(solution)/shard_map/all_to_all | solution.py:415
  31.5 7.6 %shard_map.41 = (bf16[1536,1024]{1,0:T(8,128)(2,1)S(1)}, f32[64,8]{1,0:T(8,128)S(1)}, s32[8,768]{1,0:T(8,128)S(1)}, s32[1,1]{1,0:T(1,128)}) custom-call(f32[128,4,128]{2,1,0:T(4,128)} %all-to-all-done.4.hist_ref, s32[8,768]{1,0:T(8,128)S(1)} %get-tuple-element.33.ids_ref, s32[8,896]{1,0:T(8,128)S(1)} %get-tuple-element.34.held_ref, ...), custom_call_target="tpu_custom_call" | custom-call | tf_op jit(solution)/shard_map/pallas_call | solution.py:350
  39.1 46.3 %all_to_all.45 = bf16[64,24,1024]{2,1,0:T(8,128)(2,1)S(1)} all-to-all(bf16[64,24,1024]{2,1,0:T(8,128)(2,1)S(1)} %bitcast.37), channel_id=1, replica_groups=mesh['z'=4,'y'=4,'core'=2,'x'=4] {'z','y','x'}, dimensions={0} | all-to-all | bytes 6291456 | tf_op jit(solution)/shard_map/all_to_all | solution.py:397
  85.4 0.0 copy-start
  85.4 0.0 copy-start.2
  85.4 0.0 copy-start.3
  85.4 5.8 %shard_map.42 = f32[128,128]{1,0:T(8,128)} custom-call(bf16[1536,1024]{1,0:T(8,128)(2,1)S(1)} %bitcast.36, f32[64,8]{1,0:T(8,128)S(1)} %get-tuple-element.38.ends_ref), custom_call_target="tpu_custom_call" | custom-call | tf_op jit(solution)/shard_map/pallas_call | solution.py:350
  91.2 5.4 %all-to-all-start.6 = ((f32[128,1,128]{2,1,0:T(1,128)}), f32[128,1,128]{2,1,0:T(1,128)S(1)}, u32[]{:S(2)}, u32[]{:S(2)}) async-start(f32[128,1,128]{2,1,0:T(1,128)} %bitcast.14), calls=%async_computation.6 | async-start | bytes 131072 | tf_op jit(solution)/shard_map/all_to_all | solution.py:439
  97.3 9.0 %all-to-all-done.6 = f32[128,1,128]{2,1,0:T(1,128)S(1)} async-done(((f32[128,1,128]{2,1,0:T(1,128)}), f32[128,1,128]{2,1,0:T(1,128)S(1)}, u32[]{:S(2)}, u32[]{:S(2)}) %all-to-all-start.6) | async-done | bytes 65568 | tf_op jit(solution)/shard_map/all_to_all | solution.py:439
  106.4 0.0 copy-done
  106.4 0.0 copy-done.2
  106.4 0.0 copy-done.3
  106.4 0.4 conditional.1
  106.4 0.4 branch_1_fun.1
  106.8 0.0 copy-start.4
  106.8 0.6 copy-done.4
Async XLA Ops:
  6.5 16.0 %collective-permute-start.1 = (bf16[768,1024]{1,0:T(8,128)(2,1)}, bf16[768,1024]{1,0:T(8,128)(2,1)S(1)}, u32[]{:S(2)}, u32[]{:S(2)}) collective-permute-start(bf16[768,1024]{1,0:T(8,128)(2,1)} %emb_ref.1), channel_id=1, source_target_pairs={{0,4},{4,0},{1,5},{5,1},{2,6},{6,2},{3,7},{7,3},{8,12},{12,8},{9,1... | collective-permute-start | bytes 4718600 | tf_op jit(solution)/shard_map/ppermute | solution.py:416
  9.8 21.7 %all-to-all-start.4 = ((f32[128,4,128]{2,1,0:T(4,128)}), f32[128,4,128]{2,1,0:T(4,128)}, u32[]{:S(2)}, u32[]{:S(2)}) async-start(f32[128,4,128]{2,1,0:T(4,128)} %get-tuple-element.32), calls=%async_computation.4 | async-start | bytes 524288 | tf_op jit(solution)/shard_map/all_to_all | solution.py:415
  20.5 2.1 %collective-permute-start = (s32[8,768]{1,0:T(8,128)S(1)}, s32[8,768]{1,0:T(8,128)S(1)}, u32[]{:S(2)}, u32[]{:S(2)}) collective-permute-start(s32[8,768]{1,0:T(8,128)S(1)} %get-tuple-element.33.ids_ref), channel_id=1, source_target_pairs={{0,4},{4,0},{1,5},{5,1},{2,6},{6,2},{3,7},{7,3},{8,12},{12,8},{9,1... | collective-permute-start | bytes 73736 | tf_op jit(solution)/shard_map/ppermute | solution.py:414
  85.4 21.0 %copy-start = (bf16[768,1024]{1,0:T(8,128)(2,1)S(1)}, bf16[768,1024]{1,0:T(8,128)(2,1)}, u32[]{:S(2)}) copy-start(bf16[768,1024]{1,0:T(8,128)(2,1)} %emb_ref.1) | copy-start | bytes 4718596
  85.4 21.0 %copy-start.2 = (s32[768,1]{0,1:T(1,128)S(1)}, s32[768,1]{0,1:T(1,128)}, u32[]{:S(2)}) copy-start(s32[768,1]{0,1:T(1,128)} %param.6) | copy-start | bytes 9220
  85.4 21.0 %copy-start.3 = (s32[768]{0:T(1024)S(1)}, s32[768]{0:T(1024)}, u32[]{:S(2)}) copy-start(s32[768]{0:T(1024)} %param.7) | copy-start | bytes 9220
  91.2 15.1 %all-to-all-start.6 = ((f32[128,1,128]{2,1,0:T(1,128)}), f32[128,1,128]{2,1,0:T(1,128)S(1)}, u32[]{:S(2)}, u32[]{:S(2)}) async-start(f32[128,1,128]{2,1,0:T(1,128)} %bitcast.14), calls=%async_computation.6 | async-start | bytes 131072 | tf_op jit(solution)/shard_map/all_to_all | solution.py:439
  106.8 0.6 copy-start.4

commit v3 on v2

--- a/solution.py
+++ b/solution.py
@@ -17,8 +17,8 @@
 DEVS = 128
 CAP = 24
 SLOTS = CHIPS * CAP
-TILE = 384
-HELD = 896
+LINE = 4 * CAP
+PIECE = 128
 ALL = ("z", "y", "core", "x")
 GROUP_AXES = ("z", "y", "core")
 CHIP_AXES = ("z", "y", "x")
@@ -33,10 +33,8 @@
     return lax.broadcasted_iota(jnp.int32, shape, dim)
 
 
-def dot(a, b, ca=1, cb=0, precision=None):
-    return lax.dot_general(
-        a, b, (((ca,), (cb,)), ((), ())), preferred_element_type=F32, precision=precision
-    )
+def dot(a, b, ca=1, cb=0):
+    return lax.dot_general(a, b, (((ca,), (cb,)), ((), ())), preferred_element_type=F32)
 
 
 def onehot(cond):
@@ -89,54 +87,6 @@
     return cluster & 1
 
 
-def before(flags):
-    tri = onehot(iota((256, 256), 0) < iota((256, 256), 1))
-    seen, parts = jnp.zeros((1, 1), F32), []
-    for j in range(ROWS // 256):
-        part = flags[:, j * 256 : (j + 1) * 256]
-        parts.append(dot(wide_row(part), tri)[0:1] + seen)
-        seen = seen + jnp.sum(part, axis=1, keepdims=True)
-    return jnp.concatenate(parts, axis=1), seen
-
-
-def gather_kernel(ids_ref, ids2_ref, emb_ref, emb2_ref, out_ref, ids_out_ref, raw, raw2, sems):
-    core, _ = place()
-    reads = [
-        pltpu.make_async_copy(emb_ref, raw, sems.at[0]),
-        pltpu.make_async_copy(emb2_ref, raw2, sems.at[1]),
-    ]
-    for read in reads:
-        read.start()
-    ids, ids2 = ids_ref[...], ids2_ref[...]
-    flags, flags2 = (jnp.where(parity(i[0:1]) == core, 1.0, 0.0) for i in (ids, ids2))
-    slot, total = before(flags)
-    slot2, _ = before(flags2)
-    slot = jnp.where(flags > 0, slot, -1.0)
-    slot2 = jnp.where(flags2 > 0, slot2 + total, -1.0)
-    tile = 256
-    at = iota((tile, ROWS), 0).astype(F32).astype(BF16)
-    owner_of = [
-        jnp.concatenate(
-            [(i[0:1] >> 4).astype(F32), (i[0:1] & 15).astype(F32), i[1:2].astype(F32), jnp.full((1, ROWS), 1.0 + n)]
-            + [jnp.zeros((4, ROWS), F32)],
-            axis=0,
-        ).astype(BF16)
-        for n, i in enumerate((ids, ids2))
-    ]
-    for read in reads:
-        read.wait()
-    for low in range(0, HELD, tile):
-        high = min(low + tile, HELD)
-        picks = [
-            jnp.where(jnp.clip(s - low, -1, tile).astype(BF16) == at[: high - low], BF16(1), BF16(0))
-            for s in (slot, slot2)
-        ]
-        out_ref[low:high, :] = (dot(picks[0], raw[...]) + dot(picks[1], raw2[...])).astype(BF16)
-        ids_out_ref[:, low:high] = (
-            dot(owner_of[0], picks[0], 1, 1) + dot(owner_of[1], picks[1], 1, 1)
-        ).astype(jnp.int32)
-
-
 def rotate(value, by, run=16):
     if by == 0:
         return value
@@ -168,16 +118,12 @@
     return best, turn, turned
 
 
-def placing(parts):
-    lane = iota((1, 128), 1)
-    base, sources = parts[0], [lane]
-    for part in parts[1:3]:
+def placing(parts, carried):
+    base, placed = parts[0], [carried[0]]
+    for part, rows in zip(parts[1:3], carried[1:3]):
         _, turn, (turned,) = settle(base, [part])
-        chosen = turned[0]
-        for r in range(1, 4):
-            chosen = jnp.where(turn == r, turned[r], chosen)
-        base = base + chosen
-        sources.append((lane & ~3) | ((lane - turn) & 3))
+        base = base + spun(turned, turn)
+        placed.append(spun([rotate(rows, r, 4) for r in range(4)], turn))
     loads, turns, _ = settle(base, [rotate(parts[3], 2 * c, 8) for c in range(4)])
     loads = jnp.maximum(loads, rotate(loads, 4, 8))
     best, turn, by = loads[0:1], turns[0:1], jnp.zeros((1, 128), jnp.int32)
@@ -185,10 +131,17 @@
         better = loads[c : c + 1] < best
         best = jnp.where(better, loads[c : c + 1], best)
         turn = jnp.where(better, turns[c : c + 1], turn)
-        by = jnp.where(better, 2 * c, by)
-    run = (lane & ~3) | ((lane - turn) & 3)
-    sources.append((lane & ~7) | ((run - by) & 7))
-    return jnp.max(best, axis=1, keepdims=True), sources
+        by = jnp.where(better, c, by)
+    rows = spun([rotate(carried[3], 2 * c, 8) for c in range(4)], by)
+    placed.append(spun([rotate(rows, r, 4) for r in range(4)], turn))
+    return jnp.max(best, axis=1, keepdims=True), placed
+
+
+def spun(turned, turn):
+    rows = turned[0]
+    for r in range(1, 4):
+        rows = jnp.where(turn == r, turned[r], rows)
+    return rows
 
 
 def column(weights, rows):
@@ -207,9 +160,20 @@
 
 
 def place_kernel(
-    hist_ref, ids_ref, held_ref, raw_ref, out_ref, ends_ref, rows_ref, load_ref
+    hist_ref, ids_ref, ids2_ref, emb_ref, emb2_ref, out_ref, ends_ref, rows_ref, load_ref, raw, sems
 ):
     core, chip = place()
+    reads = [
+        pltpu.make_async_copy(
+            source.at[pl.ds(n * PIECE, PIECE), :],
+            raw.at[pl.ds(i * ROWS + n * PIECE, PIECE), :],
+            sems.at[i, n],
+        )
+        for n in range(ROWS // PIECE)
+        for i, source in enumerate((emb_ref, emb2_ref))
+    ]
+    for read in reads:
+        read.start()
     hist = jnp.concatenate([hist_ref[:, j, :] for j in range(4)], axis=1).astype(BF16)
     dev = iota((CHIPS, DEVS), 1)
     first = (iota((CHIPS, DEVS), 0) >> 2) * 8 + (iota((CHIPS, DEVS), 0) & 3)
@@ -229,18 +193,15 @@
     local = iota((1, CLUSTERS), 1) & 15
     where = column((128, 16, 8, 1), (quarter, octet, local & 1, local >> 1))
 
-    wide = dot(both, same(where, iota((1, CLUSTERS), 1).astype(F32)))
-    load, sources = placing([wide[:, p * 128 : (p + 1) * 128] for p in range(4)])
-    odd = onehot(parity(iota((CLUSTERS, 128), 0)) == 1)
-    of_odd = dot(both, odd)
-    of_all = jnp.sum(both.astype(F32), axis=1, keepdims=True)
-    held = jnp.max(jnp.maximum(of_odd, of_all - of_odd), axis=0, keepdims=True)[:, 0:1]
-    load_ref[...] = jnp.where(held <= HELD, load, 2.0 * CAP).astype(jnp.int32)
-    sources = [source + p * 128 for p, source in enumerate(sources)]
-    spread = same(where, jnp.concatenate(sources, axis=1).astype(F32))
-    count0 = dot(count0.astype(BF16), spread)
-    count1 = dot(count1.astype(BF16), spread)
-
+    spread = same(where, iota((1, CLUSTERS), 1).astype(F32))
+    names = (iota((8, CLUSTERS), 1) >> 4, iota((8, CLUSTERS), 1) & 15)
+    names = jnp.where(iota((8, CLUSTERS), 0) == 0, *names).astype(F32)
+    wide = dot(jnp.concatenate([count0, count1, names], axis=0).astype(BF16), spread)
+    quarters = [wide[:, p * 128 : (p + 1) * 128] for p in range(4)]
+    load, placed = placing([w[:CHIPS] + w[CHIPS:DEVS] for w in quarters], quarters)
+    load_ref[...] = load.astype(jnp.int32)
+    placed = jnp.concatenate(placed, axis=1)
+    count0, count1, names = placed[:CHIPS], placed[CHIPS:DEVS], placed[DEVS:].astype(jnp.int32)
     at = iota((CLUSTERS, 8), 0)
     upto = iota((CLUSTERS, 8), 1)
     mine = (at & 127) == (chip >> 3) * 16 + core * 8 + (chip & 7)
@@ -258,41 +219,48 @@
     start0 = jnp.concatenate(start, axis=1)
     start1 = start0 + own0
     device_row = (iota((1, CLUSTERS), 1) & 127).astype(F32)
-    by_group = dot(in_group, spread)
-    by_local = onehot((iota((CPG, CLUSTERS), 1) & 15) == iota((CPG, CLUSTERS), 0))
-    by_local = dot(by_local, spread).astype(BF16)
+    by_group = jnp.where(names[0:1] == iota((GROUPS, CLUSTERS), 0), 1.0, 0.0)
+    by_local = onehot(names[1:2] == iota((CPG, CLUSTERS), 0))
 
     def table(row):
         return dot(by_local, (by_group * row).astype(BF16), 1, 1).astype(BF16)
 
     to_table, table0, table1 = table(device_row), table(start0), table(start1)
 
-    def slots(group, local, rank, start, rows):
-        group = onehot(group == iota((GROUPS, rows), 0))
-        local = local == iota((CPG, rows), 0)
+    def slots(ids, start):
+        group = onehot((ids[0:1] >> 4) == iota((GROUPS, ROWS), 0))
+        local = (ids[0:1] & 15) == iota((CPG, ROWS), 0)
 
         def look(table):
             return jnp.sum(jnp.where(local, dot(table, group), 0.0), axis=0, keepdims=True).astype(jnp.int32)
 
-        return look(to_table), look(start) + rank
-
-    ids = ids_ref[...]
-    first = jnp.where(core == 0, table0, table1)
-    to, k = slots(ids[0:1] >> 4, ids[0:1] & 15, ids[1:2], first, ROWS)
+        to = look(to_table)
+        k = look(start) + ids[1:2]
+        return to, k, jnp.where(((to >> 3) & 1) == core, ((to >> 4) * 8 + (to & 7)) * CAP + k, -1)
+
+    to, k, slot = slots(ids_ref[...], jnp.where(core == 0, table0, table1))
+    _, _, slot2 = slots(ids2_ref[...], jnp.where(core == 0, table1, table0))
     rows_ref[...] = jnp.concatenate([to, k, jnp.zeros((6, ROWS), jnp.int32)], axis=0)
-    held = held_ref[...]
-    group, local, rank, whose = (held[n : n + 1] for n in range(4))
-    to, k = slots(group, local, rank, first, HELD)
-    _, k2 = slots(group, local, rank, jnp.where(core == 0, table1, table0), HELD)
-    k = jnp.where(whose == 1, k, k2)
-    slot = jnp.where(whose > 0, ((to >> 4) * 8 + (to & 7)) * CAP + k, -1)
+    slot = jnp.concatenate([slot, slot2], axis=1)
+    for read in reads:
+        read.wait()
     tile = 256
-    at = iota((tile, HELD), 0).astype(F32).astype(BF16)
+    at = iota((tile, 2 * ROWS), 0).astype(F32).astype(BF16)
     for n in range(SLOTS // tile):
         pick = jnp.clip(slot - n * tile, -1, tile).astype(F32).astype(BF16)
-        rows = dot(jnp.where(pick == at, BF16(1), BF16(0)), raw_ref[...])
+        rows = dot(jnp.where(pick == at, BF16(1), BF16(0)), raw[...])
         scale = lax.rsqrt(jnp.mean(rows * rows, axis=1, keepdims=True) + 1e-06) / math.sqrt(WIDTH)
         out_ref[n * tile : (n + 1) * tile, :] = (rows * scale).astype(BF16)
+
+
+def moved(values, picks, *dims):
+    total = None
+    for _ in range(3):
+        part = values.astype(BF16)
+        values = values - part.astype(F32)
+        product = dot(part, picks, *dims)
+        total = product if total is None else total + product
+    return total
 
 
 def pairs_kernel(rows_ref, ends_ref, out_ref):
@@ -309,17 +277,20 @@
     label_row = label.astype(F32)
     order_row = (dev * 32 + k).astype(F32)
     best = []
-    for i in range(SLOTS // TILE):
-        mine = slice(i * TILE, (i + 1) * TILE)
-        top = jnp.full((1, TILE), -1.0, F32)
-        for j in range(i + 1):
-            other = slice(j * TILE, (j + 1) * TILE)
+    for low in range(0, SLOTS, 256):
+        mine = slice(low, low + 256)
+        sure, end = low // LINE * LINE, -(-(low + 256) // LINE) * LINE
+        top = jnp.full((1, 256), -1.0, F32)
+        for first, last in ((0, sure), (sure, end)):
+            if first == last:
+                continue
+            other = slice(first, last)
             score = dot(rows_ref[other, :], rows_ref[mine, :], 1, 1)
             tops = []
-            for c in range(TILE // 128):
-                part = slice(i * TILE + c * 128, i * TILE + (c + 1) * 128)
+            for c in range(2):
+                part = slice(low + c * 128, low + (c + 1) * 128)
                 keep = label_col[other] == label_row[:, part]
-                if i == j:
+                if first == sure:
                     keep = keep & (order_col[other] < order_row[:, part])
                 part = jnp.where(keep, score[:, c * 128 : (c + 1) * 128], -1.0)
                 tops.append(jnp.max(part, axis=0, keepdims=True))
@@ -328,8 +299,8 @@
     best = jnp.concatenate(best, axis=1)
     block = jnp.where(own_chip, best, 0.0)
     at = iota((SLOTS, 128), 0)
-    place_col = jnp.where(at - (at * 2731 >> 16) * CAP == iota((SLOTS, 128), 1), 1.0, 0.0)
-    found = dot(block, place_col, precision=lax.Precision.HIGHEST)
+    place_col = at - (at * 2731 >> 16) * CAP == iota((SLOTS, 128), 1)
+    found = moved(block, onehot(place_col))
     for n in range(DEVS // 8):
         four = found[n * 4 : (n + 1) * 4, :]
         out_ref[n * 8 : (n + 1) * 8, :] = jnp.concatenate([four, four], axis=0)
@@ -339,8 +310,7 @@
     to, k = rows_ref[0:1, :], rows_ref[1:2, :]
     chip = (to >> 4) * 8 + (to & 7)
     dev = (chip >> 2) * 8 + ((to >> 3) & 1) * 4 + (chip & 3)
-    pick = jnp.where(dev == iota((DEVS, ROWS), 0), 1.0, 0.0)
-    cand = dot(got_ref[:, 0:32], pick, 0, 0, precision=lax.Precision.HIGHEST)
+    cand = moved(got_ref[:, 0:32], onehot(dev == iota((DEVS, ROWS), 0)), 0, 0)
     best = jnp.sum(jnp.where(k == iota((32, ROWS), 0), cand, 0.0), axis=0, keepdims=True)
     for j in range(ROWS // 128):
         out_ref[j : j + 1, :] = best[:, j * 128 : (j + 1) * 128]
@@ -414,17 +384,6 @@
     ids2 = lax.ppermute(ids, "core", swap)
     hists = lax.all_to_all(hist, ALL, split_axis=0, concat_axis=0, tiled=True)
     embeddings2 = lax.ppermute(embeddings, "core", swap)
-    raw, held = call(
-        gather_kernel,
-        (shape(HELD, WIDTH, dtype=BF16), shape(8, HELD, dtype=jnp.int32)),
-        ids, ids2, embeddings, embeddings2,
-        in_specs=[pl.BlockSpec()] * 2 + [ANY] * 2,
-        scratch_shapes=[
-            pltpu.VMEM((ROWS, WIDTH), BF16),
-            pltpu.VMEM((ROWS, WIDTH), BF16),
-            pltpu.SemaphoreType.DMA((2,)),
-        ],
-    )
     packed, ends, places, load = call(
         place_kernel,
         (
@@ -433,7 +392,12 @@
             shape(8, ROWS, dtype=jnp.int32),
             shape(1, 1, dtype=jnp.int32),
         ),
-        hists, ids, held, raw,
+        hists, ids, ids2, embeddings, embeddings2,
+        in_specs=[pl.BlockSpec()] * 3 + [ANY] * 2,
+        scratch_shapes=[
+            pltpu.VMEM((2 * ROWS, WIDTH), BF16),
+            pltpu.SemaphoreType.DMA((2, ROWS // PIECE)),
+        ],
     )
     best = by_devices(packed, ends)
     back = lax.all_to_all(best, ALL, split_axis=0, concat_axis=0, tiled=True)

time: 115 us -> 113 us (0.983)
  waiting for transfers between devices: 13.7 us -> 19.3 us
  Pallas kernels: 20.8 us -> 15.4 us
  blocking collectives: 46.3 us -> 44.8 us
    all_to_all x1, waiting for transfers between devices: 3.82 us -> 9.36 us  [body(): hists = lax.all_to_all(hist, ALL, split_axis=0, concat_axis=0, tiled=True)]
    pallas_call x5 -> x4, Pallas kernels: 20.8 us -> 15.4 us  [call(): pl.pallas_call(kernel, out_shape=out_shape, compiler_params=pltpu.Compile...]
    all_to_all x1, blocking collectives: 46.3 us -> 44.8 us  [by_devices(): lax.all_to_all(blocks, CHIP_AXES, split_axis=0, concat_axis=0, tiled=True)]
  transfers between devices with their start and end apart: 4 -> 4, of which waited for: 3 -> 3; matrix products, arithmetic and copies ran while one was open for 0% -> 0% of each run, Pallas kernels for 6% -> 2%
where the time goes in v3:
time: 113 us; the launch traced here: 112 us
  blocking collectives  44.8 us (40%)
  waiting for transfers between devices  19.3 us (17%)
  starting transfers between devices  18.4 us (16%)
  Pallas kernels  15.4 us (14%)
  between operations  14.1 us (12%)
    all_to_all x1, blocking collectives, by_devices(): lax.all_to_all(blocks, CHIP_AXES, split_axis=0, concat_axis=0, tiled=True)  44.8 us
    pallas_call x4, Pallas kernels, call(): pl.pallas_call(kernel, out_shape=out_shape, compiler_params=pltpu.Compile...  15.4 us
    all_to_all x1, starting transfers between devices, body(): hists = lax.all_to_all(hist, ALL, split_axis=0, concat_axis=0, tiled=True)  10.2 us
    all_to_all x1, waiting for transfers between devices, body(): hists = lax.all_to_all(hist, ALL, split_axis=0, concat_axis=0, tiled=True)  9.36 us
    all_to_all x1, waiting for transfers between devices, body(): back = lax.all_to_all(best, ALL, split_axis=0, concat_axis=0, tiled=True)  9.04 us
    all_to_all x1, starting transfers between devices, body(): back = lax.all_to_all(best, ALL, split_axis=0, concat_axis=0, tiled=True)  5.59 us
  transfers between devices with their start and end apart: 4, of which 3 were waited for; matrix products, arithmetic and copies ran while one was open for 0% of the time, Pallas kernels for 2%

profile of v3, /device:TPU:1, one launch (start us, length us, event | category | flops | bytes accessed | tf_op | source)
XLA Modules:
  0.0 112.5 jit_solution(8685155157217049331)
XLA Ops:
  6.5 1.4 %collective-permute-start.1 = (bf16[768,1024]{1,0:T(8,128)(2,1)}, bf16[768,1024]{1,0:T(8,128)(2,1)S(1)}, u32[]{:S(2)}, u32[]{:S(2)}) collective-permute-start(bf16[768,1024]{1,0:T(8,128)(2,1)} %emb_ref.1), channel_id=1, source_target_pairs={{0,4},{4,0},{1,5},{5,1},{2,6},{6,2},{3,7},{7,3},{8,12},{12,8},{9,1... | collective-permute-start | bytes 4718600 | tf_op jit(solution)/shard_map/ppermute | solution.py:386
  8.0 1.9 %shard_map.39 = (f32[128,4,128]{2,1,0:T(4,128)}, s32[8,768]{1,0:T(8,128)S(1)}) custom-call(s32[1,768]{1,0:T(1,128)} %bitcast.45, s32[6,128]{1,0:T(8,128)} %bitcast.49), custom_call_target="tpu_custom_call" | custom-call | tf_op jit(solution)/shard_map/pallas_call | solution.py:320
  9.8 10.2 %all-to-all-start.4 = ((f32[128,4,128]{2,1,0:T(4,128)}), f32[128,4,128]{2,1,0:T(4,128)S(1)}, u32[]{:S(2)}, u32[]{:S(2)}) async-start(f32[128,4,128]{2,1,0:T(4,128)} %get-tuple-element.30), calls=%async_computation.4 | async-start | bytes 524288 | tf_op jit(solution)/shard_map/all_to_all | solution.py:385
  20.0 1.1 %collective-permute-start = (s32[8,768]{1,0:T(8,128)S(1)}, s32[8,768]{1,0:T(8,128)S(1)}, u32[]{:S(2)}, u32[]{:S(2)}) collective-permute-start(s32[8,768]{1,0:T(8,128)S(1)} %get-tuple-element.31.ids_ref), channel_id=1, source_target_pairs={{0,4},{4,0},{1,5},{5,1},{2,6},{6,2},{3,7},{7,3},{8,12},{12,8},{9,1... | collective-permute-start | bytes 73736 | tf_op jit(solution)/shard_map/ppermute | solution.py:384
  21.2 0.8 collective-permute-done.ids2_ref
  22.0 9.4 %all-to-all-done.4.hist_ref = f32[128,4,128]{2,1,0:T(4,128)S(1)} async-done(((f32[128,4,128]{2,1,0:T(4,128)}), f32[128,4,128]{2,1,0:T(4,128)S(1)}, u32[]{:S(2)}, u32[]{:S(2)}) %all-to-all-start.4) | async-done | bytes 262176 | tf_op jit(solution)/shard_map/all_to_all | solution.py:385
  31.4 0.0 collective-permute-done.1.emb2_ref
  31.4 8.3 %shard_map.40 = (bf16[1536,1024]{1,0:T(8,128)(2,1)S(1)}, f32[64,8]{1,0:T(8,128)S(1)}, s32[8,768]{1,0:T(8,128)S(1)}, s32[1,1]{1,0:T(1,128)}) custom-call(f32[128,4,128]{2,1,0:T(4,128)S(1)} %all-to-all-done.4.hist_ref, s32[8,768]{1,0:T(8,128)S(1)} %get-tuple-element.31.ids_ref, s32[8,768]{1,0:T(8,128)S(1)} %collective-permute-done.ids2_ref, ...), custom_call_target="tpu_custom_call" | custom-call | tf_op jit(solution)/shard_map/pallas_call | solution.py:320
  39.7 44.8 %all_to_all.45 = bf16[64,24,1024]{2,1,0:T(8,128)(2,1)S(1)} all-to-all(bf16[64,24,1024]{2,1,0:T(8,128)(2,1)S(1)} %bitcast.37), channel_id=1, replica_groups=mesh['z'=4,'y'=4,'core'=2,'x'=4] {'z','y','x'}, dimensions={0} | all-to-all | bytes 6291456 | tf_op jit(solution)/shard_map/all_to_all | solution.py:367
  84.5 0.0 copy-start
  84.5 0.0 copy-start.2
  84.5 0.0 copy-start.3
  84.5 4.9 %shard_map.41 = f32[128,128]{1,0:T(8,128)} custom-call(bf16[1536,1024]{1,0:T(8,128)(2,1)S(1)} %bitcast.36, f32[64,8]{1,0:T(8,128)S(1)} %get-tuple-element.34.ends_ref), custom_call_target="tpu_custom_call" | custom-call | tf_op jit(solution)/shard_map/pallas_call | solution.py:320
  89.4 5.6 %all-to-all-start.6 = ((f32[128,1,128]{2,1,0:T(1,128)}), f32[128,1,128]{2,1,0:T(1,128)S(1)}, u32[]{:S(2)}, u32[]{:S(2)}) async-start(f32[128,1,128]{2,1,0:T(1,128)} %bitcast.14), calls=%async_computation.6 | async-start | bytes 131072 | tf_op jit(solution)/shard_map/all_to_all | solution.py:403
  95.7 9.0 %all-to-all-done.6 = f32[128,1,128]{2,1,0:T(1,128)S(1)} async-done(((f32[128,1,128]{2,1,0:T(1,128)}), f32[128,1,128]{2,1,0:T(1,128)S(1)}, u32[]{:S(2)}, u32[]{:S(2)}) %all-to-all-start.6) | async-done | bytes 65568 | tf_op jit(solution)/shard_map/all_to_all | solution.py:403
  104.7 0.0 copy-done
  104.7 0.0 copy-done.2
  104.7 0.0 copy-done.3
  104.7 0.3 conditional.1
  104.8 0.3 branch_1_fun.1
  105.0 0.0 copy-start.4
  105.0 0.6 copy-done.4
Async XLA Ops:
  6.5 24.8 %collective-permute-start.1 = (bf16[768,1024]{1,0:T(8,128)(2,1)}, bf16[768,1024]{1,0:T(8,128)(2,1)S(1)}, u32[]{:S(2)}, u32[]{:S(2)}) collective-permute-start(bf16[768,1024]{1,0:T(8,128)(2,1)} %emb_ref.1), channel_id=1, source_target_pairs={{0,4},{4,0},{1,5},{5,1},{2,6},{6,2},{3,7},{7,3},{8,12},{12,8},{9,1... | collective-permute-start | bytes 4718600 | tf_op jit(solution)/shard_map/ppermute | solution.py:386
  9.8 21.6 %all-to-all-start.4 = ((f32[128,4,128]{2,1,0:T(4,128)}), f32[128,4,128]{2,1,0:T(4,128)S(1)}, u32[]{:S(2)}, u32[]{:S(2)}) async-start(f32[128,4,128]{2,1,0:T(4,128)} %get-tuple-element.30), calls=%async_computation.4 | async-start | bytes 524288 | tf_op jit(solution)/shard_map/all_to_all | solution.py:385
  20.0 2.0 %collective-permute-start = (s32[8,768]{1,0:T(8,128)S(1)}, s32[8,768]{1,0:T(8,128)S(1)}, u32[]{:S(2)}, u32[]{:S(2)}) collective-permute-start(s32[8,768]{1,0:T(8,128)S(1)} %get-tuple-element.31.ids_ref), channel_id=1, source_target_pairs={{0,4},{4,0},{1,5},{5,1},{2,6},{6,2},{3,7},{7,3},{8,12},{12,8},{9,1... | collective-permute-start | bytes 73736 | tf_op jit(solution)/shard_map/ppermute | solution.py:384
  84.5 20.2 %copy-start = (bf16[768,1024]{1,0:T(8,128)(2,1)S(1)}, bf16[768,1024]{1,0:T(8,128)(2,1)}, u32[]{:S(2)}) copy-start(bf16[768,1024]{1,0:T(8,128)(2,1)} %emb_ref.1) | copy-start | bytes 4718596
  84.5 20.2 %copy-start.2 = (s32[768,1]{0,1:T(1,128)S(1)}, s32[768,1]{0,1:T(1,128)}, u32[]{:S(2)}) copy-start(s32[768,1]{0,1:T(1,128)} %param.6) | copy-start | bytes 9220
  84.5 20.2 %copy-start.3 = (s32[768]{0:T(1024)S(1)}, s32[768]{0:T(1024)}, u32[]{:S(2)}) copy-start(s32[768]{0:T(1024)} %param.7) | copy-start | bytes 9220
  89.4 15.3 %all-to-all-start.6 = ((f32[128,1,128]{2,1,0:T(1,128)}), f32[128,1,128]{2,1,0:T(1,128)S(1)}, u32[]{:S(2)}, u32[]{:S(2)}) async-start(f32[128,1,128]{2,1,0:T(1,128)} %bitcast.14), calls=%async_computation.6 | async-start | bytes 131072 | tf_op jit(solution)/shard_map/all_to_all | solution.py:403
  105.0 0.6 copy-start.4

commit v4 on v3

--- a/solution.py
+++ b/solution.py
@@ -352,7 +352,12 @@
         return got.reshape((size,) + x.shape[1:])
 
     mine, ids, labels = send(unit, 0), send(global_id, -1), send(cluster, -1)
-    rows4, ids4, labels4 = (lax.all_gather(x, "x", axis=0, tiled=True) for x in (mine, ids, labels))
+
+    def of_all(x):
+        turns = [[(i, (i + by) % 4) for i in range(4)] for by in range(1, 4)]
+        return jnp.concatenate([x] + [lax.ppermute(x, "x", turn) for turn in turns], axis=0)
+
+    rows4, ids4, labels4 = of_all(mine), of_all(ids), of_all(labels)
     prod = jnp.einsum("id,jd->ij", mine, rows4, preferred_element_type=F32)
     keep = (labels[:, None] == labels4[None, :]) & (ids4[None, :] < ids[:, None])
     best = jnp.maximum(-1.0, jnp.max(jnp.where(keep, prod, -1.0), axis=1))

time: 113 us -> 99.3 us (0.88)
  between operations: 14.1 us -> 0.71 us
where the time goes in v4:
time: 99.3 us; the launch traced here: 99 us
  blocking collectives  44.8 us (45%)
  waiting for transfers between devices  19.3 us (19%)
  starting transfers between devices  18.4 us (19%)
  Pallas kernels  15.3 us (15%)
    all_to_all x1, blocking collectives, by_devices(): lax.all_to_all(blocks, CHIP_AXES, split_axis=0, concat_axis=0, tiled=True)  44.8 us
    pallas_call x4, Pallas kernels, call(): pl.pallas_call(kernel, out_shape=out_shape, compiler_params=pltpu.Compile...  15.3 us
    all_to_all x1, starting transfers between devices, body(): hists = lax.all_to_all(hist, ALL, split_axis=0, concat_axis=0, tiled=True)  10.2 us
    all_to_all x1, waiting for transfers between devices, body(): hists = lax.all_to_all(hist, ALL, split_axis=0, concat_axis=0, tiled=True)  9.36 us
    all_to_all x1, waiting for transfers between devices, body(): back = lax.all_to_all(best, ALL, split_axis=0, concat_axis=0, tiled=True)  9.04 us
    all_to_all x1, starting transfers between devices, body(): back = lax.all_to_all(best, ALL, split_axis=0, concat_axis=0, tiled=True)  5.59 us
  transfers between devices with their start and end apart: 4, of which 3 were waited for; matrix products, arithmetic and copies ran while one was open for 0% of the time, Pallas kernels for 2%

profile of v4, /device:TPU:1, one launch (start us, length us, event | category | flops | bytes accessed | tf_op | source)
XLA Modules:
  0.0 99.0 jit_solution(4810875040356387454)
XLA Ops:
  0.0 1.4 %collective-permute-start.10 = (bf16[768,1024]{1,0:T(8,128)(2,1)}, bf16[768,1024]{1,0:T(8,128)(2,1)S(1)}, u32[]{:S(2)}, u32[]{:S(2)}) collective-permute-start(bf16[768,1024]{1,0:T(8,128)(2,1)} %emb_ref.1), channel_id=1, source_target_pairs={{0,4},{4,0},{1,5},{5,1},{2,6},{6,2},{3,7},{7,3},{8,12},{12,8},{9,1... | collective-permute-start | bytes 4718600 | tf_op jit(solution)/shard_map/ppermute | solution.py:391
  1.4 1.9 %shard_map.39 = (f32[128,4,128]{2,1,0:T(4,128)}, s32[8,768]{1,0:T(8,128)S(1)}) custom-call(s32[1,768]{1,0:T(1,128)} %bitcast.40, s32[6,128]{1,0:T(8,128)} %bitcast.42), custom_call_target="tpu_custom_call" | custom-call | tf_op jit(solution)/shard_map/pallas_call | solution.py:320
  3.3 10.2 %all-to-all-start.4 = ((f32[128,4,128]{2,1,0:T(4,128)}), f32[128,4,128]{2,1,0:T(4,128)S(1)}, u32[]{:S(2)}, u32[]{:S(2)}) async-start(f32[128,4,128]{2,1,0:T(4,128)} %get-tuple-element.30), calls=%async_computation.4 | async-start | bytes 524288 | tf_op jit(solution)/shard_map/all_to_all | solution.py:390
  13.5 1.1 %collective-permute-start.9 = (s32[8,768]{1,0:T(8,128)S(1)}, s32[8,768]{1,0:T(8,128)S(1)}, u32[]{:S(2)}, u32[]{:S(2)}) collective-permute-start(s32[8,768]{1,0:T(8,128)S(1)} %get-tuple-element.31.ids_ref), channel_id=1, source_target_pairs={{0,4},{4,0},{1,5},{5,1},{2,6},{6,2},{3,7},{7,3},{8,12},{12,8},{9,1... | collective-permute-start | bytes 73736 | tf_op jit(solution)/shard_map/ppermute | solution.py:389
  14.6 0.8 collective-permute-done.9.ids2_ref
  15.5 9.4 %all-to-all-done.4.hist_ref = f32[128,4,128]{2,1,0:T(4,128)S(1)} async-done(((f32[128,4,128]{2,1,0:T(4,128)}), f32[128,4,128]{2,1,0:T(4,128)S(1)}, u32[]{:S(2)}, u32[]{:S(2)}) %all-to-all-start.4) | async-done | bytes 262176 | tf_op jit(solution)/shard_map/all_to_all | solution.py:390
  24.8 0.0 collective-permute-done.10.emb2_ref
  24.9 8.3 %shard_map.40 = (bf16[1536,1024]{1,0:T(8,128)(2,1)S(1)}, f32[64,8]{1,0:T(8,128)S(1)}, s32[8,768]{1,0:T(8,128)S(1)}, s32[1,1]{1,0:T(1,128)}) custom-call(f32[128,4,128]{2,1,0:T(4,128)S(1)} %all-to-all-done.4.hist_ref, s32[8,768]{1,0:T(8,128)S(1)} %get-tuple-element.31.ids_ref, s32[8,768]{1,0:T(8,128)S(1)} %collective-permute-done.9.ids2_ref, ...), custom_call_target="tpu_custom_call" | custom-call | tf_op jit(solution)/shard_map/pallas_call | solution.py:320
  33.2 44.8 %all_to_all.45 = bf16[64,24,1024]{2,1,0:T(8,128)(2,1)S(1)} all-to-all(bf16[64,24,1024]{2,1,0:T(8,128)(2,1)S(1)} %bitcast.32), channel_id=1, replica_groups=mesh['z'=4,'y'=4,'core'=2,'x'=4] {'z','y','x'}, dimensions={0} | all-to-all | bytes 6291456 | tf_op jit(solution)/shard_map/all_to_all | solution.py:372
  78.0 0.0 copy-start
  78.0 0.0 copy-start.1
  78.0 0.0 copy-start.2
  78.0 4.8 %shard_map.41 = f32[128,128]{1,0:T(8,128)} custom-call(bf16[1536,1024]{1,0:T(8,128)(2,1)S(1)} %bitcast.31, f32[64,8]{1,0:T(8,128)S(1)} %get-tuple-element.34.ends_ref), custom_call_target="tpu_custom_call" | custom-call | tf_op jit(solution)/shard_map/pallas_call | solution.py:320
  82.8 5.6 %all-to-all-start.6 = ((f32[128,1,128]{2,1,0:T(1,128)}), f32[128,1,128]{2,1,0:T(1,128)S(1)}, u32[]{:S(2)}, u32[]{:S(2)}) async-start(f32[128,1,128]{2,1,0:T(1,128)} %bitcast.12), calls=%async_computation.6 | async-start | bytes 131072 | tf_op jit(solution)/shard_map/all_to_all | solution.py:408
  89.1 9.0 %all-to-all-done.6 = f32[128,1,128]{2,1,0:T(1,128)S(1)} async-done(((f32[128,1,128]{2,1,0:T(1,128)}), f32[128,1,128]{2,1,0:T(1,128)S(1)}, u32[]{:S(2)}, u32[]{:S(2)}) %all-to-all-start.6) | async-done | bytes 65568 | tf_op jit(solution)/shard_map/all_to_all | solution.py:408
  98.1 0.0 copy-done
  98.1 0.0 copy-done.1
  98.1 0.0 copy-done.2
  98.1 0.3 conditional.1
  98.1 0.3 branch_1_fun.1
  98.4 0.0 copy-start.3
  98.4 0.6 copy-done.3
Async XLA Ops:
  0.0 24.8 %collective-permute-start.10 = (bf16[768,1024]{1,0:T(8,128)(2,1)}, bf16[768,1024]{1,0:T(8,128)(2,1)S(1)}, u32[]{:S(2)}, u32[]{:S(2)}) collective-permute-start(bf16[768,1024]{1,0:T(8,128)(2,1)} %emb_ref.1), channel_id=1, source_target_pairs={{0,4},{4,0},{1,5},{5,1},{2,6},{6,2},{3,7},{7,3},{8,12},{12,8},{9,1... | collective-permute-start | bytes 4718600 | tf_op jit(solution)/shard_map/ppermute | solution.py:391
  3.3 21.6 %all-to-all-start.4 = ((f32[128,4,128]{2,1,0:T(4,128)}), f32[128,4,128]{2,1,0:T(4,128)S(1)}, u32[]{:S(2)}, u32[]{:S(2)}) async-start(f32[128,4,128]{2,1,0:T(4,128)} %get-tuple-element.30), calls=%async_computation.4 | async-start | bytes 524288 | tf_op jit(solution)/shard_map/all_to_all | solution.py:390
  13.5 2.0 %collective-permute-start.9 = (s32[8,768]{1,0:T(8,128)S(1)}, s32[8,768]{1,0:T(8,128)S(1)}, u32[]{:S(2)}, u32[]{:S(2)}) collective-permute-start(s32[8,768]{1,0:T(8,128)S(1)} %get-tuple-element.31.ids_ref), channel_id=1, source_target_pairs={{0,4},{4,0},{1,5},{5,1},{2,6},{6,2},{3,7},{7,3},{8,12},{12,8},{9,1... | collective-permute-start | bytes 73736 | tf_op jit(solution)/shard_map/ppermute | solution.py:389
  78.0 20.1 %copy-start = (bf16[768,1024]{1,0:T(8,128)(2,1)S(1)}, bf16[768,1024]{1,0:T(8,128)(2,1)}, u32[]{:S(2)}) copy-start(bf16[768,1024]{1,0:T(8,128)(2,1)} %emb_ref.1) | copy-start | bytes 4718596
  78.0 20.1 %copy-start.1 = (s32[768,1]{0,1:T(1,128)S(1)}, s32[768,1]{0,1:T(1,128)}, u32[]{:S(2)}) copy-start(s32[768,1]{0,1:T(1,128)} %param.6) | copy-start | bytes 9220
  78.0 20.1 %copy-start.2 = (s32[768]{0:T(1024)S(1)}, s32[768]{0:T(1024)}, u32[]{:S(2)}) copy-start(s32[768]{0:T(1024)} %param.7) | copy-start | bytes 9220
  82.8 15.3 %all-to-all-start.6 = ((f32[128,1,128]{2,1,0:T(1,128)}), f32[128,1,128]{2,1,0:T(1,128)S(1)}, u32[]{:S(2)}, u32[]{:S(2)}) async-start(f32[128,1,128]{2,1,0:T(1,128)} %bitcast.12), calls=%async_computation.6 | async-start | bytes 131072 | tf_op jit(solution)/shard_map/all_to_all | solution.py:408
  98.4 0.6 copy-start.3

commit v5 on v4

--- a/solution.py
+++ b/solution.py
@@ -174,11 +174,8 @@
     ]
     for read in reads:
         read.start()
-    hist = jnp.concatenate([hist_ref[:, j, :] for j in range(4)], axis=1).astype(BF16)
-    dev = iota((CHIPS, DEVS), 1)
-    first = (iota((CHIPS, DEVS), 0) >> 2) * 8 + (iota((CHIPS, DEVS), 0) & 3)
-    count0 = dot(onehot(dev == first), hist)
-    count1 = dot(onehot(dev == first + 4), hist)
+    hist = jnp.concatenate([hist_ref[:, j, :] for j in range(4)], axis=1)
+    count0, count1 = hist[:CHIPS], hist[CHIPS:]
     both = (count0 + count1).astype(BF16)
 
     in_group = onehot((iota((GROUPS, CLUSTERS), 1) >> 4) == iota((GROUPS, CLUSTERS), 0))
@@ -387,7 +384,7 @@
     )
     swap = [(0, 1), (1, 0)]
     ids2 = lax.ppermute(ids, "core", swap)
-    hists = lax.all_to_all(hist, ALL, split_axis=0, concat_axis=0, tiled=True)
+    hists = lax.all_to_all(hist, ("core",) + CHIP_AXES, split_axis=0, concat_axis=0, tiled=True)
     embeddings2 = lax.ppermute(embeddings, "core", swap)
     packed, ends, places, load = call(
         place_kernel,

time: 99.3 us -> 98.7 us (level)
  no operation moved by 1% of the time
where the time goes in v5:
time: 98.7 us; the launch traced here: 98.5 us
  blocking collectives  45 us (46%)
  waiting for transfers between devices  18.8 us (19%)
  starting transfers between devices  18.2 us (18%)
  Pallas kernels  15.1 us (15%)
    all_to_all x1, blocking collectives, by_devices(): lax.all_to_all(blocks, CHIP_AXES, split_axis=0, concat_axis=0, tiled=True)  45 us
    pallas_call x4, Pallas kernels, call(): pl.pallas_call(kernel, out_shape=out_shape, compiler_params=pltpu.Compile...  15.1 us
    all_to_all x1, starting transfers between devices, body(): lax.all_to_all(hist, ('core',) + CHIP_AXES, split_axis=0, concat_axis=0,...  10.2 us
    all_to_all x1, waiting for transfers between devices, body(): back = lax.all_to_all(best, ALL, split_axis=0, concat_axis=0, tiled=True)  9.04 us
    all_to_all x1, waiting for transfers between devices, body(): lax.all_to_all(hist, ('core',) + CHIP_AXES, split_axis=0, concat_axis=0,...  8.91 us
    all_to_all x1, starting transfers between devices, body(): back = lax.all_to_all(best, ALL, split_axis=0, concat_axis=0, tiled=True)  5.45 us
  transfers between devices with their start and end apart: 4, of which 3 were waited for; matrix products, arithmetic and copies ran while one was open for 0% of the time, Pallas kernels for 2%

profile of v5, /device:TPU:1, one launch (start us, length us, event | category | flops | bytes accessed | tf_op | source)
XLA Modules:
  0.0 98.5 jit_solution(6755001312432383731)
XLA Ops:
  0.0 1.4 %collective-permute-start.10 = (bf16[768,1024]{1,0:T(8,128)(2,1)}, bf16[768,1024]{1,0:T(8,128)(2,1)S(1)}, u32[]{:S(2)}, u32[]{:S(2)}) collective-permute-start(bf16[768,1024]{1,0:T(8,128)(2,1)} %emb_ref.1), channel_id=1, source_target_pairs={{0,4},{4,0},{1,5},{5,1},{2,6},{6,2},{3,7},{7,3},{8,12},{12,8},{9,1... | collective-permute-start | bytes 4718600 | tf_op jit(solution)/shard_map/ppermute | solution.py:388
  1.4 1.9 %shard_map.39 = (f32[128,4,128]{2,1,0:T(4,128)}, s32[8,768]{1,0:T(8,128)S(1)}) custom-call(s32[1,768]{1,0:T(1,128)} %bitcast.40, s32[6,128]{1,0:T(8,128)} %bitcast.42), custom_call_target="tpu_custom_call" | custom-call | tf_op jit(solution)/shard_map/pallas_call | solution.py:317
  3.3 10.2 %all-to-all-start.4 = ((f32[128,4,128]{2,1,0:T(4,128)}), f32[128,4,128]{2,1,0:T(4,128)S(1)}, u32[]{:S(2)}, u32[]{:S(2)}) async-start(f32[128,4,128]{2,1,0:T(4,128)} %get-tuple-element.30), calls=%async_computation.4 | async-start | bytes 524288 | tf_op jit(solution)/shard_map/all_to_all | solution.py:387
  13.5 1.1 %collective-permute-start.9 = (s32[8,768]{1,0:T(8,128)S(1)}, s32[8,768]{1,0:T(8,128)S(1)}, u32[]{:S(2)}, u32[]{:S(2)}) collective-permute-start(s32[8,768]{1,0:T(8,128)S(1)} %get-tuple-element.31.ids_ref), channel_id=1, source_target_pairs={{0,4},{4,0},{1,5},{5,1},{2,6},{6,2},{3,7},{7,3},{8,12},{12,8},{9,1... | collective-permute-start | bytes 73736 | tf_op jit(solution)/shard_map/ppermute | solution.py:386
  14.6 0.8 collective-permute-done.9.ids2_ref
  15.5 8.9 %all-to-all-done.4.hist_ref = f32[128,4,128]{2,1,0:T(4,128)S(1)} async-done(((f32[128,4,128]{2,1,0:T(4,128)}), f32[128,4,128]{2,1,0:T(4,128)S(1)}, u32[]{:S(2)}, u32[]{:S(2)}) %all-to-all-start.4) | async-done | bytes 262176 | tf_op jit(solution)/shard_map/all_to_all | solution.py:387
  24.4 0.0 collective-permute-done.10.emb2_ref
  24.4 8.2 %shard_map.40 = (bf16[1536,1024]{1,0:T(8,128)(2,1)S(1)}, f32[64,8]{1,0:T(8,128)S(1)}, s32[8,768]{1,0:T(8,128)S(1)}, s32[1,1]{1,0:T(1,128)}) custom-call(f32[128,4,128]{2,1,0:T(4,128)S(1)} %all-to-all-done.4.hist_ref, s32[8,768]{1,0:T(8,128)S(1)} %get-tuple-element.31.ids_ref, s32[8,768]{1,0:T(8,128)S(1)} %collective-permute-done.9.ids2_ref, ...), custom_call_target="tpu_custom_call" | custom-call | tf_op jit(solution)/shard_map/pallas_call | solution.py:317
  32.6 45.0 %all_to_all.45 = bf16[64,24,1024]{2,1,0:T(8,128)(2,1)S(1)} all-to-all(bf16[64,24,1024]{2,1,0:T(8,128)(2,1)S(1)} %bitcast.32), channel_id=1, replica_groups=mesh['z'=4,'y'=4,'core'=2,'x'=4] {'z','y','x'}, dimensions={0} | all-to-all | bytes 6291456 | tf_op jit(solution)/shard_map/all_to_all | solution.py:369
  77.6 0.0 copy-start
  77.6 0.0 copy-start.1
  77.6 0.0 copy-start.2
  77.6 4.8 %shard_map.41 = f32[128,128]{1,0:T(8,128)} custom-call(bf16[1536,1024]{1,0:T(8,128)(2,1)S(1)} %bitcast.31, f32[64,8]{1,0:T(8,128)S(1)} %get-tuple-element.34.ends_ref), custom_call_target="tpu_custom_call" | custom-call | tf_op jit(solution)/shard_map/pallas_call | solution.py:317
  82.4 5.5 %all-to-all-start.6 = ((f32[128,1,128]{2,1,0:T(1,128)}), f32[128,1,128]{2,1,0:T(1,128)S(1)}, u32[]{:S(2)}, u32[]{:S(2)}) async-start(f32[128,1,128]{2,1,0:T(1,128)} %bitcast.12), calls=%async_computation.6 | async-start | bytes 131072 | tf_op jit(solution)/shard_map/all_to_all | solution.py:405
  88.6 9.0 %all-to-all-done.6 = f32[128,1,128]{2,1,0:T(1,128)S(1)} async-done(((f32[128,1,128]{2,1,0:T(1,128)}), f32[128,1,128]{2,1,0:T(1,128)S(1)}, u32[]{:S(2)}, u32[]{:S(2)}) %all-to-all-start.6) | async-done | bytes 65568 | tf_op jit(solution)/shard_map/all_to_all | solution.py:405
  97.6 0.0 copy-done
  97.6 0.0 copy-done.1
  97.6 0.0 copy-done.2
  97.6 0.3 conditional.1
  97.6 0.3 branch_1_fun.1
  97.9 0.0 copy-start.3
  97.9 0.6 copy-done.3
Async XLA Ops:
  0.0 24.4 %collective-permute-start.10 = (bf16[768,1024]{1,0:T(8,128)(2,1)}, bf16[768,1024]{1,0:T(8,128)(2,1)S(1)}, u32[]{:S(2)}, u32[]{:S(2)}) collective-permute-start(bf16[768,1024]{1,0:T(8,128)(2,1)} %emb_ref.1), channel_id=1, source_target_pairs={{0,4},{4,0},{1,5},{5,1},{2,6},{6,2},{3,7},{7,3},{8,12},{12,8},{9,1... | collective-permute-start | bytes 4718600 | tf_op jit(solution)/shard_map/ppermute | solution.py:388
  3.3 21.1 %all-to-all-start.4 = ((f32[128,4,128]{2,1,0:T(4,128)}), f32[128,4,128]{2,1,0:T(4,128)S(1)}, u32[]{:S(2)}, u32[]{:S(2)}) async-start(f32[128,4,128]{2,1,0:T(4,128)} %get-tuple-element.30), calls=%async_computation.4 | async-start | bytes 524288 | tf_op jit(solution)/shard_map/all_to_all | solution.py:387
  13.5 2.0 %collective-permute-start.9 = (s32[8,768]{1,0:T(8,128)S(1)}, s32[8,768]{1,0:T(8,128)S(1)}, u32[]{:S(2)}, u32[]{:S(2)}) collective-permute-start(s32[8,768]{1,0:T(8,128)S(1)} %get-tuple-element.31.ids_ref), channel_id=1, source_target_pairs={{0,4},{4,0},{1,5},{5,1},{2,6},{6,2},{3,7},{7,3},{8,12},{12,8},{9,1... | collective-permute-start | bytes 73736 | tf_op jit(solution)/shard_map/ppermute | solution.py:386
  77.6 20.0 %copy-start = (bf16[768,1024]{1,0:T(8,128)(2,1)S(1)}, bf16[768,1024]{1,0:T(8,128)(2,1)}, u32[]{:S(2)}) copy-start(bf16[768,1024]{1,0:T(8,128)(2,1)} %emb_ref.1) | copy-start | bytes 4718596
  77.6 20.0 %copy-start.1 = (s32[768,1]{0,1:T(1,128)S(1)}, s32[768,1]{0,1:T(1,128)}, u32[]{:S(2)}) copy-start(s32[768,1]{0,1:T(1,128)} %param.6) | copy-start | bytes 9220
  77.6 20.0 %copy-start.2 = (s32[768]{0:T(1024)S(1)}, s32[768]{0:T(1024)}, u32[]{:S(2)}) copy-start(s32[768]{0:T(1024)} %param.7) | copy-start | bytes 9220
  82.4 15.2 %all-to-all-start.6 = ((f32[128,1,128]{2,1,0:T(1,128)}), f32[128,1,128]{2,1,0:T(1,128)S(1)}, u32[]{:S(2)}, u32[]{:S(2)}) async-start(f32[128,1,128]{2,1,0:T(1,128)} %bitcast.12), calls=%async_computation.6 | async-start | bytes 131072 | tf_op jit(solution)/shard_map/all_to_all | solution.py:405
  97.9 0.6 copy-start.3

commit v6 on v5

--- a/solution.py
+++ b/solution.py
@@ -18,7 +18,7 @@
 CAP = 24
 SLOTS = CHIPS * CAP
 LINE = 4 * CAP
-PIECE = 128
+PIECE = 768
 ALL = ("z", "y", "core", "x")
 GROUP_AXES = ("z", "y", "core")
 CHIP_AXES = ("z", "y", "x")

time: 98.7 us -> 98.6 us (level)
  no operation moved by 1% of the time
where the time goes in v6:
time: 98.6 us; the launch traced here: 98.4 us
  blocking collectives  45 us (46%)
  waiting for transfers between devices  18.8 us (19%)
  starting transfers between devices  18.2 us (18%)
  Pallas kernels  15 us (15%)
    all_to_all x1, blocking collectives, by_devices(): lax.all_to_all(blocks, CHIP_AXES, split_axis=0, concat_axis=0, tiled=True)  45 us
    pallas_call x4, Pallas kernels, call(): pl.pallas_call(kernel, out_shape=out_shape, compiler_params=pltpu.Compile...  15 us
    all_to_all x1, starting transfers between devices, body(): lax.all_to_all(hist, ('core',) + CHIP_AXES, split_axis=0, concat_axis=0,...  10.2 us
    all_to_all x1, waiting for transfers between devices, body(): back = lax.all_to_all(best, ALL, split_axis=0, concat_axis=0, tiled=True)  9.04 us
    all_to_all x1, waiting for transfers between devices, body(): lax.all_to_all(hist, ('core',) + CHIP_AXES, split_axis=0, concat_axis=0,...  8.91 us
    all_to_all x1, starting transfers between devices, body(): back = lax.all_to_all(best, ALL, split_axis=0, concat_axis=0, tiled=True)  5.46 us
  transfers between devices with their start and end apart: 4, of which 3 were waited for; matrix products, arithmetic and copies ran while one was open for 0% of the time, Pallas kernels for 2%

profile of v6, /device:TPU:1, one launch (start us, length us, event | category | flops | bytes accessed | tf_op | source)
XLA Modules:
  0.0 98.4 jit_solution(7712914066608004174)
XLA Ops:
  0.0 1.4 %collective-permute-start.10 = (bf16[768,1024]{1,0:T(8,128)(2,1)}, bf16[768,1024]{1,0:T(8,128)(2,1)S(1)}, u32[]{:S(2)}, u32[]{:S(2)}) collective-permute-start(bf16[768,1024]{1,0:T(8,128)(2,1)} %emb_ref.1), channel_id=1, source_target_pairs={{0,4},{4,0},{1,5},{5,1},{2,6},{6,2},{3,7},{7,3},{8,12},{12,8},{9,1... | collective-permute-start | bytes 4718600 | tf_op jit(solution)/shard_map/ppermute | solution.py:388
  1.4 1.9 %shard_map.39 = (f32[128,4,128]{2,1,0:T(4,128)}, s32[8,768]{1,0:T(8,128)S(1)}) custom-call(s32[1,768]{1,0:T(1,128)} %bitcast.40, s32[6,128]{1,0:T(8,128)} %bitcast.42), custom_call_target="tpu_custom_call" | custom-call | tf_op jit(solution)/shard_map/pallas_call | solution.py:317
  3.3 10.2 %all-to-all-start.4 = ((f32[128,4,128]{2,1,0:T(4,128)}), f32[128,4,128]{2,1,0:T(4,128)S(1)}, u32[]{:S(2)}, u32[]{:S(2)}) async-start(f32[128,4,128]{2,1,0:T(4,128)} %get-tuple-element.30), calls=%async_computation.4 | async-start | bytes 524288 | tf_op jit(solution)/shard_map/all_to_all | solution.py:387
  13.5 1.1 %collective-permute-start.9 = (s32[8,768]{1,0:T(8,128)S(1)}, s32[8,768]{1,0:T(8,128)S(1)}, u32[]{:S(2)}, u32[]{:S(2)}) collective-permute-start(s32[8,768]{1,0:T(8,128)S(1)} %get-tuple-element.31.ids_ref), channel_id=1, source_target_pairs={{0,4},{4,0},{1,5},{5,1},{2,6},{6,2},{3,7},{7,3},{8,12},{12,8},{9,1... | collective-permute-start | bytes 73736 | tf_op jit(solution)/shard_map/ppermute | solution.py:386
  14.6 0.8 collective-permute-done.9.ids2_ref
  15.5 8.9 %all-to-all-done.4.hist_ref = f32[128,4,128]{2,1,0:T(4,128)S(1)} async-done(((f32[128,4,128]{2,1,0:T(4,128)}), f32[128,4,128]{2,1,0:T(4,128)S(1)}, u32[]{:S(2)}, u32[]{:S(2)}) %all-to-all-start.4) | async-done | bytes 262176 | tf_op jit(solution)/shard_map/all_to_all | solution.py:387
  24.4 0.0 collective-permute-done.10.emb2_ref
  24.4 8.0 %shard_map.40 = (bf16[1536,1024]{1,0:T(8,128)(2,1)S(1)}, f32[64,8]{1,0:T(8,128)S(1)}, s32[8,768]{1,0:T(8,128)S(1)}, s32[1,1]{1,0:T(1,128)}) custom-call(f32[128,4,128]{2,1,0:T(4,128)S(1)} %all-to-all-done.4.hist_ref, s32[8,768]{1,0:T(8,128)S(1)} %get-tuple-element.31.ids_ref, s32[8,768]{1,0:T(8,128)S(1)} %collective-permute-done.9.ids2_ref, ...), custom_call_target="tpu_custom_call" | custom-call | tf_op jit(solution)/shard_map/pallas_call | solution.py:317
  32.5 45.0 %all_to_all.45 = bf16[64,24,1024]{2,1,0:T(8,128)(2,1)S(1)} all-to-all(bf16[64,24,1024]{2,1,0:T(8,128)(2,1)S(1)} %bitcast.32), channel_id=1, replica_groups=mesh['z'=4,'y'=4,'core'=2,'x'=4] {'z','y','x'}, dimensions={0} | all-to-all | bytes 6291456 | tf_op jit(solution)/shard_map/all_to_all | solution.py:369
  77.5 0.0 copy-start
  77.5 0.0 copy-start.1
  77.5 0.0 copy-start.2
  77.5 4.8 %shard_map.41 = f32[128,128]{1,0:T(8,128)} custom-call(bf16[1536,1024]{1,0:T(8,128)(2,1)S(1)} %bitcast.31, f32[64,8]{1,0:T(8,128)S(1)} %get-tuple-element.34.ends_ref), custom_call_target="tpu_custom_call" | custom-call | tf_op jit(solution)/shard_map/pallas_call | solution.py:317
  82.3 5.5 %all-to-all-start.6 = ((f32[128,1,128]{2,1,0:T(1,128)}), f32[128,1,128]{2,1,0:T(1,128)S(1)}, u32[]{:S(2)}, u32[]{:S(2)}) async-start(f32[128,1,128]{2,1,0:T(1,128)} %bitcast.12), calls=%async_computation.6 | async-start | bytes 131072 | tf_op jit(solution)/shard_map/all_to_all | solution.py:405
  88.4 9.0 %all-to-all-done.6 = f32[128,1,128]{2,1,0:T(1,128)S(1)} async-done(((f32[128,1,128]{2,1,0:T(1,128)}), f32[128,1,128]{2,1,0:T(1,128)S(1)}, u32[]{:S(2)}, u32[]{:S(2)}) %all-to-all-start.6) | async-done | bytes 65568 | tf_op jit(solution)/shard_map/all_to_all | solution.py:405
  97.5 0.0 copy-done
  97.5 0.0 copy-done.1
  97.5 0.0 copy-done.2
  97.5 0.3 conditional.1
  97.5 0.3 branch_1_fun.1
  97.8 0.0 copy-start.3
  97.8 0.6 copy-done.3
Async XLA Ops:
  0.0 24.4 %collective-permute-start.10 = (bf16[768,1024]{1,0:T(8,128)(2,1)}, bf16[768,1024]{1,0:T(8,128)(2,1)S(1)}, u32[]{:S(2)}, u32[]{:S(2)}) collective-permute-start(bf16[768,1024]{1,0:T(8,128)(2,1)} %emb_ref.1), channel_id=1, source_target_pairs={{0,4},{4,0},{1,5},{5,1},{2,6},{6,2},{3,7},{7,3},{8,12},{12,8},{9,1... | collective-permute-start | bytes 4718600 | tf_op jit(solution)/shard_map/ppermute | solution.py:388
  3.3 21.1 %all-to-all-start.4 = ((f32[128,4,128]{2,1,0:T(4,128)}), f32[128,4,128]{2,1,0:T(4,128)S(1)}, u32[]{:S(2)}, u32[]{:S(2)}) async-start(f32[128,4,128]{2,1,0:T(4,128)} %get-tuple-element.30), calls=%async_computation.4 | async-start | bytes 524288 | tf_op jit(solution)/shard_map/all_to_all | solution.py:387
  13.5 2.0 %collective-permute-start.9 = (s32[8,768]{1,0:T(8,128)S(1)}, s32[8,768]{1,0:T(8,128)S(1)}, u32[]{:S(2)}, u32[]{:S(2)}) collective-permute-start(s32[8,768]{1,0:T(8,128)S(1)} %get-tuple-element.31.ids_ref), channel_id=1, source_target_pairs={{0,4},{4,0},{1,5},{5,1},{2,6},{6,2},{3,7},{7,3},{8,12},{12,8},{9,1... | collective-permute-start | bytes 73736 | tf_op jit(solution)/shard_map/ppermute | solution.py:386
  77.5 20.0 %copy-start = (bf16[768,1024]{1,0:T(8,128)(2,1)S(1)}, bf16[768,1024]{1,0:T(8,128)(2,1)}, u32[]{:S(2)}) copy-start(bf16[768,1024]{1,0:T(8,128)(2,1)} %emb_ref.1) | copy-start | bytes 4718596
  77.5 20.0 %copy-start.1 = (s32[768,1]{0,1:T(1,128)S(1)}, s32[768,1]{0,1:T(1,128)}, u32[]{:S(2)}) copy-start(s32[768,1]{0,1:T(1,128)} %param.6) | copy-start | bytes 9220
  77.5 20.0 %copy-start.2 = (s32[768]{0:T(1024)S(1)}, s32[768]{0:T(1024)}, u32[]{:S(2)}) copy-start(s32[768]{0:T(1024)} %param.7) | copy-start | bytes 9220
  82.3 15.2 %all-to-all-start.6 = ((f32[128,1,128]{2,1,0:T(1,128)}), f32[128,1,128]{2,1,0:T(1,128)S(1)}, u32[]{:S(2)}, u32[]{:S(2)}) async-start(f32[128,1,128]{2,1,0:T(1,128)} %bitcast.12), calls=%async_computation.6 | async-start | bytes 131072 | tf_op jit(solution)/shard_map/all_to_all | solution.py:405
  97.8 0.6 copy-start.3
